TPU v7x, 128 devices: a whole 4x4x4 slice. The times are simulated.
128 devices in a mesh: dp: 32 (over y, x, core), mp: 4 (over z).
Axes of the slice: x: 4, y: 4, z: 4, core: 2. Of those that a mesh axis runs over, the one named last changes fastest.
Arguments:
- acts: bfloat16 [8, 4096, 1024], P(None, 'dp')
- grads_out: bfloat16 [8, 4096, 16384], P(None, 'dp', 'mp')
- counts: int32 [32], replicated, may hold values from 64 to 128, as said below
- owners: int32 [32], replicated, may hold values from 0 to 31, each once
- bases_a: bfloat16 [8, 1024, 1024], P(None, 'mp'), may hold values from -0.1875 to 0.1875
- bases_g: bfloat16 [4, 32, 1024, 1024], P('mp', 'dp'), may hold values from -0.1875 to 0.1875
Outputs:
- precond: bfloat16 [8, 16, 1024, 1024], P(None, 'mp', 'dp')
Inputs may be any that keep to these rules, and one draw needn't show every extreme that they name: `owners`: every dp index owns exactly one of the 32 block positions. Rows of shard s at positions counts[s] and beyond are padding.
All inputs are finite; a program needn't handle non-finite values.
Results may differ from a plain program's by a relative error of at most 0.0065.
Values may be sent and summed in bfloat16 or wider, within the bound.
A program may use at most 128 MiB of HBM per device.

v0:
```python
import jax
import jax.numpy as jnp
from jax import lax
from jax.sharding import PartitionSpec as P

damping = 0.0001


def precondition(rows_a, rows_g, basis_a, basis_g, row_total):
    proj_a = jnp.dot(rows_a, basis_a, preferred_element_type=jnp.float32)
    proj_g = jnp.dot(rows_g, basis_g, preferred_element_type=jnp.float32)
    lam_a = jnp.sum(proj_a * proj_a, axis=0) / row_total
    lam_g = jnp.sum(proj_g * proj_g, axis=0) / row_total
    cross = (
        lax.dot_general(
            proj_a.astype(jnp.bfloat16),
            proj_g.astype(jnp.bfloat16),
            (((0,), (0,)), ((), ())),
            preferred_element_type=jnp.float32,
        )
        / row_total
    )
    scaled = (cross / (lam_a[:, None] * lam_g[None, :] + damping)).astype(jnp.bfloat16)
    right = lax.dot_general(
        scaled, basis_g, (((1,), (1,)), ((), ())), preferred_element_type=jnp.float32
    ).astype(jnp.bfloat16)
    return jnp.dot(basis_a, right, preferred_element_type=jnp.float32).astype(jnp.bfloat16)


def local(acts, grads_out, counts, owners, bases_a, bases_g):
    layer_count, tok_rows, block_size = acts.shape
    group_blocks = grads_out.shape[2] // block_size
    shard_count = lax.axis_size("dp")
    my_index = lax.axis_index("dp")
    row_total = jnp.sum(counts).astype(jnp.float32)
    live_rows = jnp.arange(tok_rows, dtype=jnp.int32) < counts[my_index]
    zero_value = jnp.zeros((), jnp.bfloat16)
    masked_acts = jnp.where(live_rows[None, :, None], acts, zero_value)
    masked_grads = jnp.where(live_rows[None, :, None], grads_out, zero_value)
    slot_ids = jnp.arange(shard_count, dtype=jnp.int32)
    inverse = jnp.sum(
        (owners[None, :] == slot_ids[:, None]).astype(jnp.int32) * slot_ids[None, :], axis=1
    )
    my_layer = inverse[my_index] // group_blocks
    layer_of_dest = inverse // group_blocks
    grad_units = (
        masked_grads.reshape(layer_count, tok_rows, group_blocks, block_size)
        .transpose(0, 2, 1, 3)
        .reshape(layer_count * group_blocks, tok_rows, block_size)
    )
    grad_send = jnp.take(grad_units, inverse, axis=0)
    layer_slice = lax.dynamic_index_in_dim(bases_a, my_layer, 0, keepdims=False)
    act_send = jnp.take(masked_acts, layer_of_dest, axis=0)
    act_recv, grad_recv = (
        lax.all_to_all(act_send, "dp", split_axis=0, concat_axis=0, tiled=True),
        lax.all_to_all(grad_send, "dp", split_axis=0, concat_axis=0, tiled=True),
    )
    basis_a = lax.all_gather(layer_slice, "mp", axis=0, tiled=True)
    rows_a = act_recv.reshape(shard_count * tok_rows, block_size)
    rows_g = grad_recv.reshape(shard_count * tok_rows, block_size)
    result_block = precondition(rows_a, rows_g, basis_a, bases_g[0, 0], row_total)
    pieces = lax.all_to_all(
        result_block.reshape(shard_count, block_size // shard_count, block_size),
        "dp",
        split_axis=0,
        concat_axis=0,
        tiled=True,
    )
    ordered = jnp.take(pieces, owners, axis=0)
    return ordered.reshape(layer_count, group_blocks, block_size // shard_count, block_size)


def solution(mesh):
    placed = (
        P(None, "dp", None),
        P(None, "dp", "mp"),
        P(),
        P(),
        P(None, "mp", None),
        P("mp", "dp", None, None),
    )
    return jax.shard_map(
        local, mesh=mesh, in_specs=placed, out_specs=P(None, "mp", "dp", None), check_vma=False
    )
```

profile of v0, /device:TPU:0, one launch (start us, length us, event | category | flops | bytes accessed | tf_op | source)
XLA Modules:
  0.0 344.5 jit_solution(15265443134902739912)
XLA Ops:
  6.5 0.0 copy-start
  6.5 0.9 select_reduce_fusion
  7.5 1.2 dynamic_slice.12
  8.7 0.6 iota_compare_fusion.1
  9.4 7.2 %broadcast_select_fusion = bf16[8,128,4096]{2,1,0:T(8,128)(2,1)} fusion(bf16[8,128,4096]{2,1,0:T(8,128)(2,1)} %param.7, pred[128]{0:T(512)(128)(4,1)S(1)} %iota_compare_fusion.1), kind=kLoop, calls=%fused_computation.9 | loop fusion | flops 4194304 | bytes 16777344 | tf_op jit(solution)/shard_map/jit(_where)/select_n | solution.py:39
  16.6 4.1 %fusion.27 = (bf16[8,128,1024]{2,1,0:T(8,128)(2,1)S(1)}, bf16[8,128,1024]{2,1,0:T(8,128)(2,1)S(1)}, bf16[8,128,1024]{2,1,0:T(8,128)(2,1)S(1)}, bf16[8,128,1024]{2,1,0:T(8,128)(2,1)S(1)}) fusion(bf16[8,128,4096]{2,1,0:T(8,128)(2,1)} %broadcast_select_fusion), kind=kLoop, calls=%fused_computation.53 | loop fusion | bytes 16777216 | tf_op jit(solution)/shard_map/slice
  20.7 3.7 %pad_maximum_fusion = bf16[8,512,1024]{2,1,0:T(8,128)(2,1)} fusion(bf16[8,128,1024]{2,1,0:T(8,128)(2,1)S(1)} %get-tuple-element.6, bf16[8,128,1024]{2,1,0:T(8,128)(2,1)S(1)} %get-tuple-element.7, bf16[8,128,1024]{2,1,0:T(8,128)(2,1)S(1)} %get-tuple-element.8, bf16[8,128,1024]{2,1,0:T(8,128)(2,1)S(1)} %get-tuple-element.5), kind=kLoop, calls=%fused_computation.5 | loop fusion | flops 33554432 | bytes 16777216 | tf_op jit(solution)/shard_map/concatenate
  24.4 8.4 %gather_fusion.1 = bf16[32,128,1024]{2,1,0:T(8,128)(2,1)} fusion(bf16[32,128,1024]{2,1,0:T(8,128)(2,1)} %bitcast.47, s32[1024]{0:T(1024)S(1)} %get-tuple-element.17), kind=kCustom, calls=%fused_computation.1 | custom fusion | bytes 16777344 | tf_op jit(solution)/shard_map/jit(_take)/gather | solution.py:51
  32.8 7.5 %broadcast_select_fusion.1 = bf16[32,128,1024]{2,1,0:T(8,128)(2,1)} fusion(bf16[32,128,1024]{2,1,0:T(8,128)(2,1)} %gather_fusion.1, pred[32]{0:T(512)(128)(4,1)S(1)} %get-tuple-element.10), kind=kLoop, calls=%fused_computation.10 | loop fusion | flops 4194304 | bytes 16777248 | tf_op jit(solution)/shard_map/jit(_take)/select_n | solution.py:51
  40.3 7.5 %all-to-all-start.1 = ((bf16[32,128,1024]{2,1,0:T(8,128)(2,1)}), bf16[32,128,1024]{2,1,0:T(8,128)(2,1)}, u32[]{:S(2)}, u32[]{:S(2)}) async-start(bf16[32,128,1024]{2,1,0:T(8,128)(2,1)} %broadcast_select_fusion.1), calls=%async_computation.1 | async-start | bytes 16777216 | tf_op jit(solution)/shard_map/all_to_all | solution.py:56
  47.8 3.1 broadcast_select_fusion.3
  50.9 6.6 %gather_fusion = bf16[32,128,1024]{2,1,0:T(8,128)(2,1)} fusion(bf16[8,128,1024]{2,1,0:T(8,128)(2,1)} %broadcast_select_fusion.3, s32[1024]{0:T(1024)S(1)} %get-tuple-element.18), kind=kCustom, calls=%fused_computation | custom fusion | bytes 16777344 | tf_op jit(solution)/shard_map/jit(_take)/gather | solution.py:53
  57.5 7.5 %broadcast_select_fusion.2 = bf16[32,128,1024]{2,1,0:T(8,128)(2,1)} fusion(bf16[32,128,1024]{2,1,0:T(8,128)(2,1)} %gather_fusion, pred[32]{0:T(512)(128)(4,1)S(1)} %get-tuple-element.9), kind=kLoop, calls=%fused_computation.11 | loop fusion | flops 4194304 | bytes 16777248 | tf_op jit(solution)/shard_map/jit(_take)/select_n | solution.py:53
  65.0 0.0 copy-start.1
  65.0 88.7 %all-to-all-done.1 = bf16[32,128,1024]{2,1,0:T(8,128)(2,1)} async-done(((bf16[32,128,1024]{2,1,0:T(8,128)(2,1)}), bf16[32,128,1024]{2,1,0:T(8,128)(2,1)}, u32[]{:S(2)}, u32[]{:S(2)}) %all-to-all-start.1) | async-done | bytes 8388640 | tf_op jit(solution)/shard_map/all_to_all | solution.py:56
  153.7 5.0 %all-to-all-start = ((bf16[32,128,1024]{2,1,0:T(8,128)(2,1)}), bf16[32,128,1024]{2,1,0:T(8,128)(2,1)}, u32[]{:S(2)}, u32[]{:S(2)}) async-start(bf16[32,128,1024]{2,1,0:T(8,128)(2,1)} %broadcast_select_fusion.2), calls=%async_computation | async-start | bytes 16777216 | tf_op jit(solution)/shard_map/all_to_all | solution.py:55
  158.7 0.2 all-gather.3.cloned.1.call-start
  158.9 0.6 dynamic_slice.10
  162.1 1.9 constant_dynamic-slice_fusion
  164.0 0.0 all-gather.3.cloned.1.call-update
  164.0 0.0 copy-done.1
  164.0 0.7 reduce_sum.40
  165.4 0.0 copy-done
  165.4 14.6 %multiply_reduce_fusion = (f32[1024]{0:T(1024)S(1)}, bf16[4096,1024]{1,0:T(8,128)(2,1)}) fusion(bf16[4096,1024]{1,0:T(8,128)(2,1)} %bitcast.8, bf16[1,1,1024,1024]{3,2,1,0:T(8,128)(2,1)S(1)} %copy-done), kind=kOutput, calls=%fused_computation.3 | convolution fusion | flops 8602516480 | bytes 18878464 | tf_op jit(solution)/shard_map/dot_general | solution.py:11
  180.0 17.6 %all-gather.3.cloned.1.call-done = bf16[1,1024,1024]{2,1,0:T(8,128)(2,1)} async-done(((bf16[1,256,1024]{2,1,0:T(8,128)(2,1)}), bf16[1,1024,1024]{2,1,0:T(8,128)(2,1)}) %all-gather.3.cloned.1.call-update) | async-done | bytes 2097168 | tf_op jit(solution)/shard_map/all_gather | solution.py:58
  197.6 67.0 %all-to-all-done = bf16[32,128,1024]{2,1,0:T(8,128)(2,1)} async-done(((bf16[32,128,1024]{2,1,0:T(8,128)(2,1)}), bf16[32,128,1024]{2,1,0:T(8,128)(2,1)}, u32[]{:S(2)}, u32[]{:S(2)}) %all-to-all-start) | async-done | bytes 8388640 | tf_op jit(solution)/shard_map/all_to_all | solution.py:55
  264.6 0.0 copy-start.3
  264.6 13.0 %multiply_reduce_fusion.1 = (f32[1024]{0:T(1024)S(1)}, bf16[4096,1024]{1,0:T(8,128)(2,1)S(1)}) fusion(bf16[4096,1024]{1,0:T(8,128)(2,1)} %bitcast.5, bf16[1,1024,1024]{2,1,0:T(8,128)(2,1)} %all-gather.3.cloned.1.call-done), kind=kOutput, calls=%fused_computation.4 | convolution fusion | flops 8602516480 | bytes 18878464 | tf_op jit(solution)/shard_map/dot_general | solution.py:10
  277.6 0.0 copy-done.3
  277.6 10.4 %divide_convert_fusion = bf16[1024,1024]{1,0:T(8,128)(2,1)} fusion(bf16[4096,1024]{1,0:T(8,128)(2,1)S(1)} %copy-done.3, bf16[4096,1024]{1,0:T(8,128)(2,1)S(1)} %get-tuple-element.16, f32[1024]{0:T(1024)S(1)} %broadcast_divide_fusion, f32[1024]{0:T(1024)S(1)} %broadcast_divide_fusion.1, f32[]{:T(128)S(6)} %convert_element_type.21), kind=kOutput, calls=%fused_computation.12 | convolution fusion | flops 8595177472 | bytes 18882564 | tf_op jit(solution)/shard_map/dot_general | solution.py:15
  288.0 8.1 %fusion.16 = bf16[1024,1024]{1,0:T(8,128)(2,1)} fusion(bf16[1,1024,1024]{2,1,0:T(8,128)(2,1)} %all-gather.3.cloned.1.call-done, bf16[1024,1024]{1,0:T(8,128)(2,1)} %divide_convert_fusion, bf16[1,1,1024,1024]{3,2,1,0:T(8,128)(2,1)S(1)} %copy-done), kind=kOutput, calls=%fused_computation.24 | convolution fusion | flops 4297064448 | bytes 8388608 | tf_op jit(solution)/shard_map/dot_general | solution.py:27
  296.1 0.0 copy-start.2
  296.1 4.9 %all-to-all-start.2 = ((bf16[32,32,1024]{2,1,0:T(8,128)(2,1)}), bf16[32,32,1024]{2,1,0:T(8,128)(2,1)}, u32[]{:S(2)}, u32[]{:S(2)}) async-start(bf16[32,32,1024]{2,1,0:T(8,128)(2,1)} %bitcast.49), calls=%async_computation.2 | async-start | bytes 4194304 | tf_op jit(solution)/shard_map/all_to_all | solution.py:62
  301.0 0.0 copy-done.2
  301.0 0.1 broadcast_in_dim.63
  301.1 29.8 %all-to-all-done.2 = bf16[32,32,1024]{2,1,0:T(8,128)(2,1)} async-done(((bf16[32,32,1024]{2,1,0:T(8,128)(2,1)}), bf16[32,32,1024]{2,1,0:T(8,128)(2,1)}, u32[]{:S(2)}, u32[]{:S(2)}) %all-to-all-start.2) | async-done | bytes 2097184 | tf_op jit(solution)/shard_map/all_to_all | solution.py:62
  330.9 3.6 %gather_fusion.2 = bf16[32,32,1024]{2,1,0:T(8,128)(2,1)} fusion(bf16[32,32,1024]{2,1,0:T(8,128)(2,1)} %all-to-all-done.2, s32[1024]{0:T(1024)S(1)} %pad_clamp_fusion), kind=kCustom, calls=%fused_computation.2 | custom fusion | bytes 4194432 | tf_op jit(solution)/shard_map/jit(_take)/gather | solution.py:69
  334.5 3.2 broadcast_select_fusion.4
  (8 shorter events, 0.1 us)
Async XLA Ops:
  6.5 158.9 %copy-start = (bf16[1,1,1024,1024]{3,2,1,0:T(8,128)(2,1)S(1)}, bf16[1,1,1024,1024]{3,2,1,0:T(8,128)(2,1)}, u32[]{:S(2)}) copy-start(bf16[1,1,1024,1024]{3,2,1,0:T(8,128)(2,1)} %param.11) | copy-start | bytes 6291460
  40.3 113.4 %all-to-all-start.1 = ((bf16[32,128,1024]{2,1,0:T(8,128)(2,1)}), bf16[32,128,1024]{2,1,0:T(8,128)(2,1)}, u32[]{:S(2)}, u32[]{:S(2)}) async-start(bf16[32,128,1024]{2,1,0:T(8,128)(2,1)} %broadcast_select_fusion.1), calls=%async_computation.1 | async-start | bytes 16777216 | tf_op jit(solution)/shard_map/all_to_all | solution.py:56
  65.0 99.0 %copy-start.1 = (s32[32]{0:T(128)S(1)}, s32[32]{0:T(128)}, u32[]{:S(2)}) copy-start(s32[32]{0:T(128)} %param.8) | copy-start | bytes 388
  153.7 110.9 %all-to-all-start = ((bf16[32,128,1024]{2,1,0:T(8,128)(2,1)}), bf16[32,128,1024]{2,1,0:T(8,128)(2,1)}, u32[]{:S(2)}, u32[]{:S(2)}) async-start(bf16[32,128,1024]{2,1,0:T(8,128)(2,1)} %broadcast_select_fusion.2), calls=%async_computation | async-start | bytes 16777216 | tf_op jit(solution)/shard_map/all_to_all | solution.py:55
  158.7 38.9 %all-gather.3.cloned.1.call-start = ((), (), s32[]{:S(2)}) async-start(), calls=%async_computation.3 | async-start | bytes 2621440 | tf_op jit(solution)/shard_map/all_gather | solution.py:58
  264.6 13.0 %copy-start.3 = (bf16[4096,1024]{1,0:T(8,128)(2,1)S(1)}, bf16[4096,1024]{1,0:T(8,128)(2,1)}, u32[]{:S(2)}) copy-start(bf16[4096,1024]{1,0:T(8,128)(2,1)} %get-tuple-element.14) | copy-start | bytes 25165828
  296.1 4.9 %copy-start.2 = (s32[32]{0:T(128)S(1)}, s32[32]{0:T(128)}, u32[]{:S(2)}) copy-start(s32[32]{0:T(128)} %param.9) | copy-start | bytes 388
  296.1 34.9 %all-to-all-start.2 = ((bf16[32,32,1024]{2,1,0:T(8,128)(2,1)}), bf16[32,32,1024]{2,1,0:T(8,128)(2,1)}, u32[]{:S(2)}, u32[]{:S(2)}) async-start(bf16[32,32,1024]{2,1,0:T(8,128)(2,1)} %bitcast.49), calls=%async_computation.2 | async-start | bytes 4194304 | tf_op jit(solution)/shard_map/all_to_all | solution.py:62
Sparse Core Ops, SparseCore 0:
  164.1 33.4 all-gather.2
where the time goes:
time: 345 us
  waiting for transfers between devices  203 us (59%)
  matrix products  46.1 us (13%)
  other arithmetic  34.5 us (10%)
  local copies, waits for them, and re-layouts  26.4 us (8%)
  starting transfers between devices  17.6 us (5%)
  between operations  16.8 us (5%)
    all_to_all x1, waiting for transfers between devices, local(): lax.all_to_all(grad_send, 'dp', split_axis=0, concat_axis=0, tiled=True)  88.7 us
    all_to_all x1, waiting for transfers between devices, local(): lax.all_to_all(act_send, 'dp', split_axis=0, concat_axis=0, tiled=True)  67 us
    all_to_all x1, waiting for transfers between devices, local(): lax.all_to_all(result_block.reshape(shard_count, block_size // shard_coun...  29.8 us
    all_gather x1, waiting for transfers between devices, local(): basis_a = lax.all_gather(layer_slice, 'mp', axis=0, tiled=True)  17.6 us
    dot_general x1, matrix products, precondition(): proj_g = jnp.dot(rows_g, basis_g, preferred_element_type=jnp.float32)  14.6 us
    dot_general x1, matrix products, precondition(): proj_a = jnp.dot(rows_a, basis_a, preferred_element_type=jnp.float32)  13 us
    dot_general x1, matrix products, precondition(): lax.dot_general(proj_a.astype(jnp.bfloat16), proj_g.astype(jnp.bfloat16),...  10.4 us
    gather x1, local copies, waits for them, and re-layouts, local(): grad_send = jnp.take(grad_units, inverse, axis=0)  8.4 us
  transfers between devices with their start and end apart: 4, of which 4 were waited for; matrix products, arithmetic and copies ran while one was open for 10% of the time, Pallas kernels for 0%

commit v1 on v0

v1 whole, which is shorter than its diff:
```python
import functools

import jax
import jax.numpy as jnp
from jax import lax
from jax.experimental import pallas as pl
from jax.experimental.pallas import tpu as pltpu
from jax.sharding import PartitionSpec as P

MESH = pl.DeviceIdType.MESH
damping = 0.0001
BLK = 1024
TILE = 256
NY, NX, NC, NZ = 4, 4, 2, 4
N_DP = NY * NX * NC
HALF = 64
SUB = HALF // NZ

PAIRS = [(2, 2), (1, 3), (3, 1), (2, 0), (0, 2), (1, 1), (3, 3), (2, 1), (2, 3), (1, 2), (3, 2), (0, 1), (1, 0), (0, 3), (3, 0)]
SPREAD = [(dy, dx, dc) for dc in range(NC) for dy, dx in PAIRS] + [(0, 0, 1)]
SLOTS = (1, 3, 2)


def kernel(
    inv_ref, own_ref, cnt_ref, acts_hbm, grads_hbm, ba_hbm, bg_hbm, out_hbm,
    graw, araw, baraw, bg, first, mid, rows, sa, ra, proj, basis, lam, lam_a, lam_g, cross, back, mask,
    load_sem, act_send, act_recv, ba_send, ba_recv, lam_send, lam_recv,
    p1_send, p1_recv, p1e_send, p1e_recv, p2_send, p2_recv, z_send, z_recv, zf_send, zf_recv, out_send, out_recv, store_sem,
):
    me, mz = lax.axis_index("dp"), lax.axis_index("mp")
    my, mx, mc = me // 8, (me // 2) % 4, me % 2

    def at(dy, dx, dc):
        return ((my + dy) % NY) * 8 + ((mx + dx) % NX) * 2 + (mc + dc) % NC

    def zat(dz):
        return (me, (mz + dz) % NZ)

    def send(src, dst, ssem, rsem, target):
        copy = pltpu.make_async_remote_copy(
            src_ref=src, dst_ref=dst, send_sem=ssem, recv_sem=rsem, device_id=target, device_id_type=MESH
        )
        copy.start()
        return copy

    loads = [
        pltpu.make_async_copy(acts_hbm.at[:, pl.ds(mz * SUB, SUB)], araw.at[:, 0], load_sem.at[0]),
        pltpu.make_async_copy(acts_hbm.at[:, pl.ds(HALF + mz * SUB, SUB)], araw.at[:, 1], load_sem.at[1]),
        pltpu.make_async_copy(ba_hbm, baraw, load_sem.at[2]),
    ]
    for j in range(4):
        loads.append(
            pltpu.make_async_copy(grads_hbm.at[:, :, pl.ds(j * BLK, BLK)], graw.at[:, j], load_sem.at[3 + j])
        )
    loads.append(pltpu.make_async_copy(bg_hbm, bg, load_sem.at[7]))
    for copy in loads:
        copy.start()

    barrier = pltpu.get_barrier_semaphore()
    peers = [(at(*d), mz) for d in SPREAD] + [zat(dz) for dz in (1, 2, 3)]
    for peer in peers:
        pl.semaphore_signal(barrier, inc=1, device_id=peer, device_id_type=MESH)

    live = cnt_ref[me] - HALF
    row_ids = lax.broadcasted_iota(jnp.int32, (HALF, BLK), 0)
    mask[...] = jnp.where(row_ids < live, 1.0, 0.0).astype(jnp.bfloat16)

    loads[0].wait()
    loads[1].wait()
    pl.semaphore_wait(barrier, len(peers))

    sub_mask = mask[pl.ds(pl.multiple_of(mz * SUB, SUB), SUB), :]

    def pack_acts(dst, index, disp):
        layer = inv_ref[at(*disp)] // 4
        dst[index, pl.ds(0, SUB), :] = araw[layer, 0]
        dst[index, pl.ds(SUB, SUB), :] = araw[layer, 1] * sub_mask

    def index_of(dy, dx, dc):
        return (dy * 4 + dx) * 2 + dc

    act_copies = []
    for disp in SPREAD:
        i = index_of(*disp)
        pack_acts(sa, i, disp)
        act_copies.append(send(sa.at[i], ra.at[i], act_send.at[i], act_recv.at[i], (at(*disp), mz)))
    pack_acts(ra, 0, (0, 0, 0))

    loads[2].wait()
    basis[mz] = baraw[inv_ref[me] // 4]
    ba_copies = [
        send(basis.at[mz], basis.at[mz], ba_send.at[k], ba_recv.at[k], zat(dz)) for k, dz in enumerate(SLOTS)
    ]

    for j in range(4):
        loads[3 + j].wait()

    def disp_of(half, slot, e):
        other, dc = e // 2, e % 2
        return (other, slot, dc) if half == 0 else (slot, other, dc)

    def hop(half, slot):
        return (at(0, slot, 0) if half == 0 else at(slot, 0, 0), mz)

    def pack(half, disp):
        unit = inv_ref[at(*disp)]
        block = graw[unit // 4, unit % 4, pl.ds(half * HALF, HALF), :]
        return block if half == 0 else block * mask[...]

    p1, p1e, p2 = {}, {}, {}
    for slot in SLOTS:
        for half in range(2):
            for e in range(8):
                first[half, slot - 1, e] = pack(half, disp_of(half, slot, e))
            p1[half, slot] = send(
                first.at[half, slot - 1, pl.ds(1, 7)], mid.at[half, slot],
                p1_send.at[half, slot], p1_recv.at[half, slot], hop(half, slot),
            )
            p1e[half, slot] = send(
                first.at[half, slot - 1, 0], rows.at[(half * 4 + slot) * 8],
                p1e_send.at[half, slot], p1e_recv.at[half, slot], hop(half, slot),
            )

    def forward(half, slot):
        for e in (4, 5, 2, 6, 3, 7, 1):
            disp = (e // 2, 0, e % 2) if half == 0 else (0, e // 2, e % 2)
            p2[half, slot, e] = send(
                mid.at[half, slot, e - 1], rows.at[(half * 4 + slot) * 8 + e],
                p2_send.at[half, slot, e], p2_recv.at[half, slot, e], (at(*disp), mz),
            )

    for half in range(2):
        for e in range(1, 8):
            mid[half, 0, e - 1] = pack(half, disp_of(half, 0, e))
        rows[half * 32] = pack(half, disp_of(half, 0, 0))
        forward(half, 0)

    for copy in act_copies:
        copy.wait_recv()
    for copy in ba_copies:
        copy.wait_recv()
    lam[mz] = jnp.zeros((8, BLK), jnp.float32)

    def proj_a_step(step, carry):
        dy, cols = step // 4, pl.ds(pl.multiple_of((step % 4) * TILE, TILE), TILE)
        block = ra[pl.ds(dy * 8, 8)].reshape(256, BLK)
        value = jnp.dot(
            block, basis[:, :, cols].reshape(BLK, TILE), preferred_element_type=jnp.float32
        )
        lam[mz, :, cols] += jnp.sum((value * value).reshape(32, 8, TILE), axis=0)
        value = value.astype(jnp.bfloat16)
        for dx in range(4):
            for dc in range(2):
                r = (dx * 2 + dc) * 32
                proj[dx * 8 + dy * 2 + dc, mz, :, cols] = value[r : r + SUB]
                proj[(4 + dy) * 8 + dx * 2 + dc, mz, :, cols] = value[r + SUB : r + 2 * SUB]
        return carry

    lax.fori_loop(0, 16, proj_a_step, 0)

    z_copies = {}
    for k, dz in enumerate((1, 3)):
        z_copies[dz] = send(proj.at[:, mz], proj.at[:, mz], z_send.at[k], z_recv.at[k], zat(dz))
    lam_copies = [send(lam.at[mz], lam.at[mz], lam_send.at[k], lam_recv.at[k], zat(dz)) for k, dz in enumerate(SLOTS)]

    for slot in (1, 3):
        for half in range(2):
            p1[half, slot].wait_recv()
            forward(half, slot)
    for half in range(2):
        p1[half, 2].wait_recv()
        forward(half, 2)

    z_copies[1].wait_recv()
    below = (mz + 3) % NZ
    zf = [send(proj.at[pl.ds(0, 32), below], proj.at[pl.ds(0, 32), below], zf_send.at[0], zf_recv.at[0], zat(1))]
    z_copies[3].wait_recv()
    above = (mz + 1) % NZ
    zf.append(send(proj.at[pl.ds(32, 32), above], proj.at[pl.ds(32, 32), above], zf_send.at[1], zf_recv.at[1], zat(3)))

    loads[7].wait()
    lam_g[...] = jnp.zeros_like(lam_g)
    cross[...] = jnp.zeros_like(cross)

    def proj_g(half, slot):
        for e in range(8):
            if slot == 0 and e == 0:
                continue
            (p1e[half, slot] if e == 0 else p2[half, slot, e]).wait_recv()
        g = half * 4 + slot

        def step(n, carry):
            cols = pl.ds(pl.multiple_of(n * TILE, TILE), TILE)
            value = jnp.dot(
                rows[pl.ds(g * 8, 8)].reshape(512, BLK), bg[:, cols], preferred_element_type=jnp.float32
            )
            lam_g[:, cols] += jnp.sum((value * value).reshape(64, 8, TILE), axis=0)
            graw[g, :, :, cols] = value.astype(jnp.bfloat16).reshape(4, 128, TILE)
            return carry

        lax.fori_loop(0, 4, step, 0)

    def cross_step(step, carry):
        g, p, q = step // 8, (step // 2) % 4, step % 2
        prows = pl.ds(pl.multiple_of(p * TILE, TILE), TILE)
        cols = pl.ds(pl.multiple_of(q * 512, 512), 512)
        left = proj[pl.ds(g * 8, 8), :, :, prows].reshape(512, TILE)
        cross[prows, cols] += lax.dot_general(
            left, graw[g, :, :, cols].reshape(512, 512), (((0,), (0,)), ((), ())), preferred_element_type=jnp.float32
        )
        return carry

    for slot in (0, 1, 3):
        for half in range(2):
            proj_g(half, slot)
    for copy in zf:
        copy.wait_recv()
    for copy in lam_copies:
        copy.wait_recv()
    for g0, g1 in ((0, 2), (3, 6), (7, 8)):
        lax.fori_loop(g0 * 8, g1 * 8, cross_step, 0)
    proj_g(0, 2)
    lax.fori_loop(2 * 8, 3 * 8, cross_step, 0)
    proj_g(1, 2)
    lax.fori_loop(6 * 8, 7 * 8, cross_step, 0)

    total = cnt_ref[0]
    for s in range(1, N_DP):
        total += cnt_ref[s]
    row_total = total.astype(jnp.float32)

    sum_a = jnp.sum(lam[0] + lam[1] + lam[2] + lam[3], axis=0, keepdims=True)
    lam_a[...] = jnp.broadcast_to(sum_a, (8, BLK)) / row_total
    lam_g[...] = jnp.broadcast_to(jnp.sum(lam_g[...], axis=0, keepdims=True), (8, BLK)) / row_total

    def right_step(p, carry):
        prows = pl.ds(pl.multiple_of(p * TILE, TILE), TILE)
        col_a = jnp.transpose(lam_a[:, prows], (1, 0))[:, 0:1]
        scaled = (cross[prows, :] / row_total) / (col_a * lam_g[0:1, :] + damping)
        scaled = scaled.astype(jnp.bfloat16)
        for n in range(4):
            baraw[4 + p, :, n * TILE : (n + 1) * TILE] = lax.dot_general(
                scaled, bg[n * TILE : (n + 1) * TILE, :], (((1,), (1,)), ((), ())), preferred_element_type=jnp.float32
            ).astype(jnp.bfloat16)
        return carry

    lax.fori_loop(0, 4, right_step, 0)

    for copy in act_copies:
        copy.wait_send()

    def out_step(step, carry):
        t, cols = step // 4, pl.ds(pl.multiple_of((step % 4) * TILE, TILE), TILE)
        value = jnp.dot(
            basis[t], baraw[pl.ds(4, 4), :, cols].reshape(BLK, TILE), preferred_element_type=jnp.float32
        )
        sa[pl.ds(t * 8, 8), :, cols] = value.astype(jnp.bfloat16).reshape(8, 32, TILE)
        return carry

    lax.fori_loop(0, 16, out_step, 0)
    out_copies = []
    for disp in SPREAD:
        i, target = index_of(*disp), at(*disp)
        out_copies.append(send(sa.at[target], back.at[me], out_send.at[i], out_recv.at[i], (target, mz)))
    back[me] = sa[me]
    for copy in out_copies:
        copy.wait_recv()
    stores = []
    for part in range(4):
        for u in range(part * 8, part * 8 + 8):
            ra[u] = back[own_ref[u]]
        stores.append(
            pltpu.make_async_copy(ra.at[pl.ds(part * 8, 8)], out_hbm.at[pl.ds(part * 8, 8)], store_sem.at[part])
        )
        stores[-1].start()
    for copy in stores:
        copy.wait()
    for copy in out_copies + ba_copies + lam_copies + zf + list(z_copies.values()):
        copy.wait_send()
    for copies in (p1, p1e, p2):
        for copy in copies.values():
            copy.wait_send()


def local(acts, grads_out, counts, owners, bases_a, bases_g):
    slot_ids = jnp.arange(N_DP, dtype=jnp.int32)
    inverse = jnp.sum((owners[None, :] == slot_ids[:, None]).astype(jnp.int32) * slot_ids[None, :], axis=1)
    smem = pl.BlockSpec(memory_space=pltpu.SMEM)
    hbm = pl.BlockSpec(memory_space=pl.ANY)
    bf16, f32 = jnp.bfloat16, jnp.float32
    dma = pltpu.SemaphoreType.DMA
    result = pl.pallas_call(
        kernel,
        out_shape=jax.ShapeDtypeStruct((N_DP, 32, BLK), bf16),
        in_specs=[smem, smem, smem, hbm, hbm, hbm, hbm],
        out_specs=hbm,
        scratch_shapes=[
            pltpu.VMEM((8, 4, 128, BLK), bf16),
            pltpu.VMEM((8, 2, SUB, BLK), bf16),
            pltpu.VMEM((8, 256, BLK), bf16),
            pltpu.VMEM((BLK, BLK), bf16),
            pltpu.VMEM((2, 3, 8, HALF, BLK), bf16),
            pltpu.VMEM((2, 4, 7, HALF, BLK), bf16),
            pltpu.VMEM((64, HALF, BLK), bf16),
            pltpu.VMEM((N_DP, 32, BLK), bf16),
            pltpu.VMEM((N_DP, 32, BLK), bf16),
            pltpu.VMEM((64, NZ, SUB, BLK), bf16),
            pltpu.VMEM((NZ, 256, BLK), bf16),
            pltpu.VMEM((NZ, 8, BLK), f32),
            pltpu.VMEM((8, BLK), f32),
        pltpu.VMEM((8, BLK), f32),
            pltpu.VMEM((BLK, BLK), f32),
            pltpu.VMEM((N_DP, 32, BLK), bf16),
            pltpu.VMEM((HALF, BLK), bf16),
            dma((8,)),
            dma((N_DP,)), dma((N_DP,)),
            dma((3,)), dma((3,)),
            dma((3,)), dma((3,)),
            dma((2, 4)), dma((2, 4)),
            dma((2, 4)), dma((2, 4)),
            dma((2, 4, 8)), dma((2, 4, 8)),
            dma((2,)), dma((2,)),
            dma((2,)), dma((2,)),
            dma((N_DP,)), dma((N_DP,)),
            dma((4,)),
        ],
        compiler_params=pltpu.CompilerParams(
            collective_id=0, has_side_effects=True, vmem_limit_bytes=63 * 1024 * 1024
        ),
        name="kfac",
    )(inverse, owners, counts, acts, grads_out, bases_a, bases_g.reshape(BLK, BLK))
    return result.reshape(8, 4, 32, BLK)


def solution(mesh):
    placed = (
        P(None, "dp", None),
        P(None, "dp", "mp"),
        P(),
        P(),
        P(None, "mp", None),
        P("mp", "dp", None, None),
    )
    return jax.shard_map(
        local, mesh=mesh, in_specs=placed, out_specs=P(None, "mp", "dp", None), check_vma=False
    )
```

time: 345 us -> 187 us (0.54)
  waiting for transfers between devices: 203 us -> 0 us
  Pallas kernels: 0 us -> 181 us
  matrix products: 46.1 us -> 0 us
  other arithmetic: 34.5 us -> 1.28 us
  local copies, waits for them, and re-layouts: 26.4 us -> 3.19 us
  starting transfers between devices: 17.6 us -> 0 us
  between operations: 16.8 us -> 0.01 us
    all_to_all x3 -> x0, waiting for transfers between devices: 185 us -> none  [the longest x1 88.7 us: local(): lax.all_to_all(grad_send, 'dp', split_axis=0, concat_axis=0, tiled=True)]
    pallas_call x0 -> x1, Pallas kernels: none -> 181 us  [local(): pl.pallas_call(kernel, out_shape=jax.ShapeDtypeStruct((N_DP, 32, BLK), bf...]
    dot_general x4 -> x0, matrix products: 46.1 us -> none  [the longest x1 14.6 us: precondition(): proj_g = jnp.dot(rows_g, basis_g, preferred_element_type=jnp.float32)]
    select_n x7 -> x0, other arithmetic: 28.5 us -> none  [the longest x2 7.49 us: local(): act_send = jnp.take(masked_acts, layer_of_dest, axis=0)]
    gather x3 -> x0, local copies, waits for them, and re-layouts: 18.6 us -> none  [the longest x1 8.4 us: local(): grad_send = jnp.take(grad_units, inverse, axis=0)]
    all_gather x1 -> x0, waiting for transfers between devices: 17.6 us -> none  [local(): basis_a = lax.all_gather(layer_slice, 'mp', axis=0, tiled=True)]
    all_to_all x3 -> x0, starting transfers between devices: 17.4 us -> none  [the longest x1 7.53 us: local(): lax.all_to_all(grad_send, 'dp', split_axis=0, concat_axis=0, tiled=True)]
    slice x1 -> x0, local copies, waits for them, and re-layouts: 4.05 us -> none
  transfers between devices with their start and end apart: 4 -> 0, of which waited for: 4 -> 0; matrix products, arithmetic and copies ran while one was open for 10% -> 0% of each run, Pallas kernels for 0% -> 0%
where the time goes in v1:
time: 187 us; the launch traced here: 185 us
  Pallas kernels  181 us (97%)
  local copies, waits for them, and re-layouts  3.19 us (2%)
    pallas_call x1, Pallas kernels, local(): pl.pallas_call(kernel, out_shape=jax.ShapeDtypeStruct((N_DP, 32, BLK), bf...  181 us

profile of v1, /device:TPU:0, one launch (start us, length us, event | category | flops | bytes accessed | tf_op | source)
XLA Modules:
  0.0 185.5 jit_solution(17897942212912703484)
XLA Ops:
  0.0 1.3 select_reduce_fusion.inv_ref
  1.3 181.0 %kfac.1 = bf16[32,32,1024]{2,1,0:T(8,128)(2,1)} custom-call(s32[32]{0:T(128)} %select_reduce_fusion.inv_ref, s32[32]{0:T(128)} %own_ref.1, s32[32]{0:T(128)} %cnt_ref.1, bf16[8,128,1024]{2,1,0:T(8,128)(2,1)} %acts_hbm.1, bf16[8,128,4096]{2,1,0:T(8,128)(2,1)} %grads_hbm.1, bf16[8,256,1024]{2,1,0:T(8,128)(2,1)} %ba_hbm.1, bf16[1024,1024]{1,0:T(8,128)(2,1)} %bitcast.3), custom_call_target="tpu_custom_call" | custom-call | tf_op jit(solution)/shard_map/kfac/pallas_call | solution.py:292
  182.3 3.2 %copy.8 = bf16[8,4,32,1024]{3,2,1,0:T(8,128)(2,1)} copy(bf16[8,4,32,1024]{3,2,1,0:T(8,128)(2,1)} %bitcast.2) | data formatting | bytes 4194304

commit v2 on v1

v2 whole, which is shorter than its diff:
```python
import functools

import jax
import jax.numpy as jnp
from jax import lax
from jax.experimental import pallas as pl
from jax.experimental.pallas import tpu as pltpu
from jax.sharding import PartitionSpec as P

MESH = pl.DeviceIdType.MESH
damping = 0.0001
BLK = 1024
TILE = 256
HCOL = 512
NY, NX, NC, NZ = 4, 4, 2, 4
N_DP = NY * NX * NC
HALF = 64
SUB = HALF // NZ

PAIRS = [(2, 2), (1, 3), (3, 1), (2, 0), (0, 2), (1, 1), (3, 3), (2, 1), (2, 3), (1, 2), (3, 2), (0, 1), (1, 0), (0, 3), (3, 0)]
SPREAD = [(dy, dx, dc) for dc in range(NC) for dy, dx in PAIRS] + [(0, 0, 1)]
SLOTS = (1, 3, 2)


def kernel(
    inv_ref, own_ref, cnt_ref, acts_hbm, grads_hbm, ba_hbm, bg_hbm, out_hbm,
    graw, araw, baraw, bg, first, mid, rows, sa, ra, proj, basis, lam, lam_g, cross, back, mask,
    load_sem, act_send, act_recv, ba_send, ba_recv, lam_send, lam_recv,
    p1_send, p1_recv, p1e_send, p1e_recv, p2_send, p2_recv, z_send, z_recv, zf_send, zf_recv, out_send, out_recv, store_sem,
):
    me, mz = lax.axis_index("dp"), lax.axis_index("mp")
    my, mx, mc = me // 8, (me // 2) % 4, me % 2

    def at(dy, dx, dc):
        return ((my + dy) % NY) * 8 + ((mx + dx) % NX) * 2 + (mc + dc) % NC

    def zat(dz):
        return (me, (mz + dz) % NZ)

    def send(src, dst, ssem, rsem, target):
        copy = pltpu.make_async_remote_copy(
            src_ref=src, dst_ref=dst, send_sem=ssem, recv_sem=rsem, device_id=target, device_id_type=MESH
        )
        copy.start()
        return copy

    loads = [
        pltpu.make_async_copy(acts_hbm.at[:, pl.ds(mz * SUB, SUB)], araw.at[:, 0], load_sem.at[0]),
        pltpu.make_async_copy(acts_hbm.at[:, pl.ds(HALF + mz * SUB, SUB)], araw.at[:, 1], load_sem.at[1]),
        pltpu.make_async_copy(ba_hbm, baraw, load_sem.at[2]),
    ]
    for j in range(8):
        loads.append(
            pltpu.make_async_copy(grads_hbm.at[:, :, pl.ds(j * HCOL, HCOL)], graw.at[j], load_sem.at[3 + j])
        )
    loads.append(pltpu.make_async_copy(bg_hbm, bg, load_sem.at[11]))
    for copy in loads:
        copy.start()

    barrier = pltpu.get_barrier_semaphore()
    peers = [(at(*d), mz) for d in SPREAD] + [zat(dz) for dz in (1, 2, 3)]
    for peer in peers:
        pl.semaphore_signal(barrier, inc=1, device_id=peer, device_id_type=MESH)

    live = cnt_ref[me] - HALF
    row_ids = lax.broadcasted_iota(jnp.int32, (HALF, BLK), 0)
    mask[...] = jnp.where(row_ids < live, 1.0, 0.0).astype(jnp.bfloat16)

    loads[0].wait()
    loads[1].wait()
    pl.semaphore_wait(barrier, len(peers))

    sub_mask = mask[pl.ds(pl.multiple_of(mz * SUB, SUB), SUB), :]

    def pack_acts(dst, index, disp):
        layer = inv_ref[at(*disp)] // 4
        dst[index, pl.ds(0, SUB), :] = araw[layer, 0]
        dst[index, pl.ds(SUB, SUB), :] = araw[layer, 1] * sub_mask

    def index_of(dy, dx, dc):
        return (dy * 4 + dx) * 2 + dc

    act_copies = []
    for disp in SPREAD:
        i = index_of(*disp)
        pack_acts(sa, i, disp)
        act_copies.append(send(sa.at[i], ra.at[i], act_send.at[i], act_recv.at[i], (at(*disp), mz)))
    pack_acts(ra, 0, (0, 0, 0))

    loads[2].wait()
    basis[mz] = baraw[inv_ref[me] // 4]
    ba_copies = [
        send(basis.at[mz], basis.at[mz], ba_send.at[k], ba_recv.at[k], zat(dz)) for k, dz in enumerate(SLOTS)
    ]

    for j in range(8):
        loads[3 + j].wait()

    def disp_of(half, slot, e):
        other, dc = e // 2, e % 2
        return (other, slot, dc) if half == 0 else (slot, other, dc)

    def hop(half, slot):
        return (at(0, slot, 0) if half == 0 else at(slot, 0, 0), mz)

    def pack(dst, half, disp):
        unit = inv_ref[at(*disp)]
        layer, column = unit // 4, unit % 4
        for c in range(2):
            cols = pl.ds(c * HCOL, HCOL)
            block = graw[column * 2 + c, layer, pl.ds(half * HALF, HALF), :]
            dst[:, cols] = block if half == 0 else block * mask[:, cols]

    p1, p1e, p2 = {}, {}, {}
    def forward(half, slot):
        for e in (4, 5, 2, 6, 3, 7, 1):
            disp = (e // 2, 0, e % 2) if half == 0 else (0, e // 2, e % 2)
            p2[half, slot, e] = send(
                mid.at[half, slot, e - 1], rows.at[(half * 4 + slot) * 8 + e],
                p2_send.at[half, slot, e], p2_recv.at[half, slot, e], (at(*disp), mz),
            )

    def start_slot(slot):
        for half in range(2):
            for e in range(8):
                pack(first.at[half, slot - 1, e], half, disp_of(half, slot, e))
            p1[half, slot] = send(
                first.at[half, slot - 1, pl.ds(1, 7)], mid.at[half, slot],
                p1_send.at[half, slot], p1_recv.at[half, slot], hop(half, slot),
            )
            p1e[half, slot] = send(
                first.at[half, slot - 1, 0], rows.at[(half * 4 + slot) * 8],
                p1e_send.at[half, slot], p1e_recv.at[half, slot], hop(half, slot),
            )

    for half in range(2):
        for e in range(1, 8):
            pack(mid.at[half, 0, e - 1], half, disp_of(half, 0, e))
        pack(rows.at[half * 32], half, disp_of(half, 0, 0))
        forward(half, 0)
    start_slot(1)
    start_slot(3)
    start_slot(2)

    loads[11].wait()
    for k in range(4):
        baraw[k] = jnp.transpose(bg[:, k * TILE : (k + 1) * TILE], (1, 0))

    for copy in act_copies:
        copy.wait_recv()
    for copy in ba_copies:
        copy.wait_recv()
    lam[mz] = jnp.zeros((8, BLK), jnp.float32)
    lam_g[...] = jnp.zeros_like(lam_g)
    cross[...] = jnp.zeros_like(cross)

    def proj_a_step(step, carry):
        block = ra[pl.ds(step * 16, 16)].reshape(512, BLK)
        value = jnp.dot(block, basis[...].reshape(BLK, BLK), preferred_element_type=jnp.float32)
        lam[mz] += jnp.sum((value * value).reshape(64, 8, BLK), axis=0)
        value = value.astype(jnp.bfloat16)
        for y in range(2):
            dy = step * 2 + y
            for dx in range(4):
                for dc in range(2):
                    r = (y * 8 + dx * 2 + dc) * 32
                    proj[dx * 8 + dy * 2 + dc, mz] = value[r : r + SUB]
                    proj[(4 + dy) * 8 + dx * 2 + dc, mz] = value[r + SUB : r + 2 * SUB]
        return carry

    lax.fori_loop(0, 2, proj_a_step, 0)

    z_copies = {}
    for k, dz in enumerate((1, 3)):
        z_copies[dz] = send(proj.at[:, mz], proj.at[:, mz], z_send.at[k], z_recv.at[k], zat(dz))
    lam_copies = [send(lam.at[mz], lam.at[mz], lam_send.at[k], lam_recv.at[k], zat(dz)) for k, dz in enumerate(SLOTS)]

    for slot in (1, 3):
        for half in range(2):
            p1[half, slot].wait_recv()
            forward(half, slot)
    for half in range(2):
        p1[half, 2].wait_recv()
        forward(half, 2)

    z_copies[1].wait_recv()
    below = (mz + 3) % NZ
    zf = [send(proj.at[pl.ds(0, 32), below], proj.at[pl.ds(0, 32), below], zf_send.at[0], zf_recv.at[0], zat(1))]
    z_copies[3].wait_recv()
    above = (mz + 1) % NZ
    zf.append(send(proj.at[pl.ds(32, 32), above], proj.at[pl.ds(32, 32), above], zf_send.at[1], zf_recv.at[1], zat(3)))

    def proj_g(half, slot):
        for e in range(8):
            if slot == 0 and e == 0:
                continue
            (p1e[half, slot] if e == 0 else p2[half, slot, e]).wait_recv()
        g = half * 4 + slot
        value = lax.dot_general(
            baraw[pl.ds(0, 4)].reshape(BLK, BLK), rows[pl.ds(g * 8, 8)].reshape(512, BLK),
            (((1,), (1,)), ((), ())), preferred_element_type=jnp.float32,
        )
        square = value * value
        lam_g[...] += square[:, 0:128] + square[:, 128:256] + square[:, 256:384] + square[:, 384:512]
        graw[g] = value.astype(jnp.bfloat16).reshape(8, 128, HCOL)

    def cross_part(g, part):
        return jnp.dot(
            graw[g, pl.ds(part * 4, 4)].reshape(512, HCOL), proj[pl.ds(g * 8, 8)].reshape(512, BLK),
            preferred_element_type=jnp.float32,
        )

    def add_cross(half, slot):
        for part in range(2):
            cross[pl.ds(part * 512, 512), :] += cross_part(half * 4 + slot, part)

    for slot in (0, 1, 3):
        for half in range(2):
            proj_g(half, slot)
    for copy in zf + lam_copies:
        copy.wait_recv()
    for slot in (0, 1, 3):
        for half in range(2):
            add_cross(half, slot)
    proj_g(0, 2)
    add_cross(0, 2)
    proj_g(1, 2)

    total = cnt_ref[0]
    for s in range(1, N_DP):
        total += cnt_ref[s]
    row_total = total.astype(jnp.float32)
    row_a = jnp.sum(lam[0] + lam[1] + lam[2] + lam[3], axis=0, keepdims=True) / row_total
    col_g = jnp.sum(lam_g[...], axis=1, keepdims=True) / row_total
    for part in range(2):
        prows = slice(part * 512, part * 512 + 512)
        value = (cross[prows, :] + cross_part(6, part)) / row_total
        scaled = value / (col_g[prows] * row_a + damping)
        baraw[4 + part * 2 : 6 + part * 2] = scaled.astype(jnp.bfloat16).reshape(2, 256, BLK)

    for copies in (act_copies, p1.values(), p1e.values()):
        for copy in copies:
            copy.wait_send()

    out_copies = []
    for part in range(2):
        prows, cols = pl.ds(part * 512, 512), pl.ds(part * HCOL, HCOL)
        first[0, part] = jnp.dot(
            bg[prows, :], baraw[pl.ds(4, 4)].reshape(BLK, BLK), preferred_element_type=jnp.float32
        ).astype(jnp.bfloat16).reshape(8, HALF, BLK)
        sa[:, :, cols] = lax.dot_general(
            basis[...].reshape(BLK, BLK), first[0, part].reshape(512, BLK), (((1,), (1,)), ((), ())),
            preferred_element_type=jnp.float32,
        ).astype(jnp.bfloat16).reshape(N_DP, 32, HCOL)
        for disp in SPREAD:
            i, target = index_of(*disp), at(*disp)
            out_copies.append(
                send(
                    sa.at[target, :, cols], back.at[me, :, cols],
                    out_send.at[part, i], out_recv.at[part, i], (target, mz),
                )
            )
    back[me] = sa[me]
    for copy in out_copies:
        copy.wait_recv()
    stores = []
    for part in range(4):
        for u in range(part * 8, part * 8 + 8):
            ra[u] = back[own_ref[u]]
        stores.append(
            pltpu.make_async_copy(ra.at[pl.ds(part * 8, 8)], out_hbm.at[pl.ds(part * 8, 8)], store_sem.at[part])
        )
        stores[-1].start()
    for copy in stores:
        copy.wait()
    for copy in out_copies + ba_copies + lam_copies + zf + list(z_copies.values()) + list(p2.values()):
        copy.wait_send()


def local(acts, grads_out, counts, owners, bases_a, bases_g):
    slot_ids = jnp.arange(N_DP, dtype=jnp.int32)
    inverse = jnp.sum((owners[None, :] == slot_ids[:, None]).astype(jnp.int32) * slot_ids[None, :], axis=1)
    smem = pl.BlockSpec(memory_space=pltpu.SMEM)
    hbm = pl.BlockSpec(memory_space=pl.ANY)
    bf16, f32 = jnp.bfloat16, jnp.float32
    dma = pltpu.SemaphoreType.DMA
    result = pl.pallas_call(
        kernel,
        out_shape=jax.ShapeDtypeStruct((N_DP, 32, BLK), bf16),
        in_specs=[smem, smem, smem, hbm, hbm, hbm, hbm],
        out_specs=hbm,
        scratch_shapes=[
            pltpu.VMEM((8, 8, 128, HCOL), bf16),
            pltpu.VMEM((8, 2, SUB, BLK), bf16),
            pltpu.VMEM((8, 256, BLK), bf16),
            pltpu.VMEM((BLK, BLK), bf16),
            pltpu.VMEM((2, 3, 8, HALF, BLK), bf16),
            pltpu.VMEM((2, 4, 7, HALF, BLK), bf16),
            pltpu.VMEM((64, HALF, BLK), bf16),
            pltpu.VMEM((N_DP, 32, BLK), bf16),
            pltpu.VMEM((N_DP, 32, BLK), bf16),
            pltpu.VMEM((64, NZ, SUB, BLK), bf16),
            pltpu.VMEM((NZ, 256, BLK), bf16),
            pltpu.VMEM((NZ, 8, BLK), f32),
            pltpu.VMEM((BLK, 128), f32),
            pltpu.VMEM((BLK, BLK), f32),
            pltpu.VMEM((N_DP, 32, BLK), bf16),
            pltpu.VMEM((HALF, BLK), bf16),
            dma((12,)),
            dma((N_DP,)), dma((N_DP,)),
            dma((3,)), dma((3,)),
            dma((3,)), dma((3,)),
            dma((2, 4)), dma((2, 4)),
            dma((2, 4)), dma((2, 4)),
            dma((2, 4, 8)), dma((2, 4, 8)),
            dma((2,)), dma((2,)),
            dma((2,)), dma((2,)),
            dma((2, N_DP)), dma((2, N_DP)),
            dma((4,)),
        ],
        compiler_params=pltpu.CompilerParams(
            collective_id=0, has_side_effects=True, vmem_limit_bytes=63 * 1024 * 1024
        ),
        name="kfac",
    )(inverse, owners, counts, acts, grads_out, bases_a, bases_g.reshape(BLK, BLK))
    return result.reshape(8, 4, 32, BLK)


def solution(mesh):
    placed = (
        P(None, "dp", None),
        P(None, "dp", "mp"),
        P(),
        P(),
        P(None, "mp", None),
        P("mp", "dp", None, None),
    )
    return jax.shard_map(
        local, mesh=mesh, in_specs=placed, out_specs=P(None, "mp", "dp", None), check_vma=False
    )
```

time: 187 us -> 165 us (0.88)
  Pallas kernels: 181 us -> 160 us
    pallas_call x1, Pallas kernels: 181 us -> 160 us  [local(): pl.pallas_call(kernel, out_shape=jax.ShapeDtypeStruct((N_DP, 32, BLK), bf...]
where the time goes in v2:
time: 165 us; the launch traced here: 164 us
  Pallas kernels  160 us (97%)
  local copies, waits for them, and re-layouts  3.19 us (2%)
    pallas_call x1, Pallas kernels, local(): pl.pallas_call(kernel, out_shape=jax.ShapeDtypeStruct((N_DP, 32, BLK), bf...  160 us

profile of v2, /device:TPU:0, one launch (start us, length us, event | category | flops | bytes accessed | tf_op | source)
XLA Modules:
  0.0 164.4 jit_solution(5126967790345499954)
XLA Ops:
  0.0 1.3 select_reduce_fusion.inv_ref
  1.3 159.9 %kfac.1 = bf16[32,32,1024]{2,1,0:T(8,128)(2,1)} custom-call(s32[32]{0:T(128)} %select_reduce_fusion.inv_ref, s32[32]{0:T(128)} %own_ref.1, s32[32]{0:T(128)} %cnt_ref.1, bf16[8,128,1024]{2,1,0:T(8,128)(2,1)} %acts_hbm.1, bf16[8,128,4096]{2,1,0:T(8,128)(2,1)} %grads_hbm.1, bf16[8,256,1024]{2,1,0:T(8,128)(2,1)} %ba_hbm.1, bf16[1024,1024]{1,0:T(8,128)(2,1)} %bitcast.3), custom_call_target="tpu_custom_call" | custom-call | tf_op jit(solution)/shard_map/kfac/pallas_call | solution.py:287
  161.2 3.2 %copy.8 = bf16[8,4,32,1024]{3,2,1,0:T(8,128)(2,1)} copy(bf16[8,4,32,1024]{3,2,1,0:T(8,128)(2,1)} %bitcast.2) | data formatting | bytes 4194304

commit v3 on v2

v3 whole, which is shorter than its diff:
```python
import functools

import jax
import jax.numpy as jnp
from jax import lax
from jax.experimental import pallas as pl
from jax.experimental.pallas import tpu as pltpu
from jax.sharding import PartitionSpec as P

MESH = pl.DeviceIdType.MESH
damping = 0.0001
BLK = 1024
TILE = 256
HCOL = 512
NY, NX, NC, NZ = 4, 4, 2, 4
N_DP = NY * NX * NC
HALF = 64
SUB = HALF // NZ

PAIRS = [(2, 2), (1, 3), (3, 1), (2, 0), (0, 2), (1, 1), (3, 3), (2, 1), (2, 3), (1, 2), (3, 2), (0, 1), (1, 0), (0, 3), (3, 0)]
SPREAD = [(dy, dx, dc) for dc in range(NC) for dy, dx in PAIRS] + [(0, 0, 1)]
SLOTS = (1, 3, 2)
SECOND = [(0, 0), (0, 1), (2, 0), (2, 1), (1, 0), (3, 0), (1, 1), (3, 1)]
COLS = 256


def kernel(
    own_ref, cnt_ref, acts_hbm, grads_hbm, ba_hbm, bg_hbm, out_hbm,
    graw, araw, baraw, bg, first, mid, rows, sa, ra, proj, basis, lam, lam_g, cross, mask, inv_ref,
    load_sem, act_send, act_recv, ba_send, ba_recv, lam_send, lam_recv,
    p1_send, p1_recv, p1e_send, p1e_recv, p2_send, p2_recv, z_send, z_recv, zf_send, zf_recv, out_send, out_recv, store_sem,
):
    me, mz = lax.axis_index("dp"), lax.axis_index("mp")
    my, mx, mc = me // 8, (me // 2) % 4, me % 2

    def at(dy, dx, dc):
        return ((my + dy) % NY) * 8 + ((mx + dx) % NX) * 2 + (mc + dc) % NC

    def zat(dz):
        return (me, (mz + dz) % NZ)

    def send(src, dst, ssem, rsem, target):
        copy = pltpu.make_async_remote_copy(
            src_ref=src, dst_ref=dst, send_sem=ssem, recv_sem=rsem, device_id=target, device_id_type=MESH
        )
        copy.start()
        return copy

    loads = [
        pltpu.make_async_copy(acts_hbm.at[:, pl.ds(mz * SUB, SUB)], araw.at[:, 0], load_sem.at[0]),
        pltpu.make_async_copy(acts_hbm.at[:, pl.ds(HALF + mz * SUB, SUB)], araw.at[:, 1], load_sem.at[1]),
    ]
    for j in range(8):
        loads.append(
            pltpu.make_async_copy(grads_hbm.at[:, :, pl.ds(j * HCOL, HCOL)], graw.at[j], load_sem.at[2 + j])
        )
    loads.append(pltpu.make_async_copy(ba_hbm, baraw, load_sem.at[10]))
    loads.append(pltpu.make_async_copy(bg_hbm, bg, load_sem.at[11]))
    for copy in loads:
        copy.start()

    barrier = pltpu.get_barrier_semaphore()
    peers = [(at(*d), mz) for d in SPREAD] + [zat(dz) for dz in (1, 2, 3)]
    for peer in peers:
        pl.semaphore_signal(barrier, inc=1, device_id=peer, device_id_type=MESH)

    def invert(d, carry):
        unit = jnp.int32(0)
        for u in range(1, N_DP):
            unit = jnp.where(own_ref[u] == d, u, unit)
        inv_ref[d] = unit
        return carry

    lax.fori_loop(0, N_DP, invert, 0)

    live = cnt_ref[me] - HALF
    row_ids = lax.broadcasted_iota(jnp.int32, (HALF, BLK), 0)
    mask[...] = jnp.where(row_ids < live, 1.0, 0.0).astype(jnp.bfloat16)

    sub_mask = mask[pl.ds(pl.multiple_of(mz * SUB, SUB), SUB), :]

    def pack_acts(dst, index, disp):
        layer = inv_ref[at(*disp)] // 4
        dst[index, pl.ds(0, SUB), :] = araw[layer, 0]
        dst[index, pl.ds(SUB, SUB), :] = araw[layer, 1] * sub_mask

    def index_of(dy, dx, dc):
        return (dy * 4 + dx) * 2 + dc

    loads[0].wait()
    loads[1].wait()
    for disp in SPREAD:
        pack_acts(sa, index_of(*disp), disp)
    pack_acts(ra, 0, (0, 0, 0))

    def disp_of(half, slot, e):
        other, dc = SECOND[e]
        return (other, slot, dc) if half == 0 else (slot, other, dc)

    def hop(half, slot):
        return (at(0, slot, 0) if half == 0 else at(slot, 0, 0), mz)

    def pack(dst, half, disp):
        unit = inv_ref[at(*disp)]
        layer, column = unit // 4, unit % 4
        for c in range(2):
            cols = pl.ds(c * HCOL, HCOL)
            block = graw[column * 2 + c, layer, pl.ds(half * HALF, HALF), :]
            dst[:, cols] = block if half == 0 else block * mask[:, cols]

    p1, p1e, p2 = {}, {}, {}

    def forward(half, slot):
        for e in range(2, 9):
            e = 1 if e == 8 else e
            other, dc = SECOND[e]
            p2[half, slot, e] = send(
                mid.at[half, slot, e - 1], rows.at[(half * 4 + slot) * 8 + e],
                p2_send.at[half, slot, e], p2_recv.at[half, slot, e],
                (at(other, 0, dc) if half == 0 else at(0, other, dc), mz),
            )

    def pack_slot(slot):
        for half in range(2):
            for e in range(8):
                pack(first.at[half, slot - 1, e], half, disp_of(half, slot, e))

    def start_slot(slot):
        for half in range(2):
            p1[half, slot] = send(
                first.at[half, slot - 1, pl.ds(1, 7)], mid.at[half, slot],
                p1_send.at[half, slot], p1_recv.at[half, slot], hop(half, slot),
            )
            p1e[half, slot] = send(
                first.at[half, slot - 1, 0], rows.at[(half * 4 + slot) * 8],
                p1e_send.at[half, slot], p1e_recv.at[half, slot], hop(half, slot),
            )

    for j in range(8):
        loads[2 + j].wait()
    for half in range(2):
        for e in range(1, 8):
            pack(mid.at[half, 0, e - 1], half, disp_of(half, 0, e))
        pack(rows.at[half * 32], half, disp_of(half, 0, 0))
    loads[10].wait()
    basis[mz] = baraw[inv_ref[me] // 4]

    pl.semaphore_wait(barrier, len(peers))
    act_copies = []
    for disp in SPREAD:
        i = index_of(*disp)
        act_copies.append(send(sa.at[i], ra.at[i], act_send.at[i], act_recv.at[i], (at(*disp), mz)))
    ba_copies = [
        send(basis.at[mz], basis.at[mz], ba_send.at[k], ba_recv.at[k], zat(dz)) for k, dz in enumerate(SLOTS)
    ]
    forward(0, 0)
    forward(1, 0)
    for slot in SLOTS:
        pack_slot(slot)
        start_slot(slot)

    loads[11].wait()
    for k in range(4):
        baraw[k] = jnp.transpose(bg[:, k * TILE : (k + 1) * TILE], (1, 0))

    for copy in act_copies:
        copy.wait_recv()
    for copy in ba_copies:
        copy.wait_recv()
    lam[mz] = jnp.zeros((8, BLK), jnp.float32)
    lam_g[...] = jnp.zeros_like(lam_g)
    cross[...] = jnp.zeros_like(cross)

    def proj_a_step(step, carry):
        block = ra[pl.ds(step * 16, 16)].reshape(512, BLK)
        value = jnp.dot(block, basis[...].reshape(BLK, BLK), preferred_element_type=jnp.float32)
        lam[mz] += jnp.sum((value * value).reshape(64, 8, BLK), axis=0)
        value = value.astype(jnp.bfloat16)
        for y in range(2):
            dy = step * 2 + y
            for dx in range(4):
                for dc in range(2):
                    r = (y * 8 + dx * 2 + dc) * 32
                    e = 2 * step + dc if y == 0 else 4 + step + 2 * dc
                    proj[dx * 8 + e, mz] = value[r : r + SUB]
                    proj[(4 + dy) * 8 + SECOND.index((dx, dc)), mz] = value[r + SUB : r + 2 * SUB]
        return carry

    lax.fori_loop(0, 2, proj_a_step, 0)

    z_copies = {}
    for k, dz in enumerate((1, 3)):
        z_copies[dz] = send(proj.at[:, mz], proj.at[:, mz], z_send.at[k], z_recv.at[k], zat(dz))
    lam_copies = [send(lam.at[mz], lam.at[mz], lam_send.at[k], lam_recv.at[k], zat(dz)) for k, dz in enumerate(SLOTS)]

    for slot in (1, 3):
        for half in range(2):
            p1[half, slot].wait_recv()
            forward(half, slot)
    for half in range(2):
        p1[half, 2].wait_recv()
        forward(half, 2)

    z_copies[1].wait_recv()
    below = (mz + 3) % NZ
    zf = [send(proj.at[pl.ds(0, 32), below], proj.at[pl.ds(0, 32), below], zf_send.at[0], zf_recv.at[0], zat(1))]
    z_copies[3].wait_recv()
    above = (mz + 1) % NZ
    zf.append(send(proj.at[pl.ds(32, 32), above], proj.at[pl.ds(32, 32), above], zf_send.at[1], zf_recv.at[1], zat(3)))

    def arrived(half, slot, blocks):
        for e in blocks:
            if slot == 0 and e == 0:
                continue
            (p1e[half, slot] if e == 0 else p2[half, slot, e]).wait_recv()

    def project(block):
        value = lax.dot_general(
            baraw[pl.ds(0, 4)].reshape(BLK, BLK), block, (((1,), (1,)), ((), ())), preferred_element_type=jnp.float32
        )
        square = value * value
        part = square[:, 0:128]
        for k in range(1, block.shape[0] // 128):
            part += square[:, k * 128 : (k + 1) * 128]
        lam_g[...] += part
        return value.astype(jnp.bfloat16)

    def proj_g(slot, count):
        def step(half, carry):
            g = half * 4 + slot
            value = project(rows[pl.ds(g * 8, count)].reshape(count * HALF, BLK))
            graw[g, :, :, pl.ds(0, count * HALF)] = value.reshape(8, 128, count * HALF)
            return carry

        for half in range(2):
            arrived(half, slot, range(count))
        lax.fori_loop(0, 2, step, 0)

    def add_cross(slot, count):
        def step(i, carry):
            half, part = i // 2, i % 2
            g = half * 4 + slot
            right = proj[pl.ds(g * 8, count)].reshape(count * HALF, BLK)
            left = graw[g, pl.ds(part * 4, 4), :, pl.ds(0, count * HALF)].reshape(512, count * HALF)
            prows = pl.ds(pl.multiple_of(part * 512, 512), 512)
            cross[prows, :] += jnp.dot(left, right, preferred_element_type=jnp.float32)
            return carry

        lax.fori_loop(0, 4, step, 0)

    for slot in (0, 1, 3):
        proj_g(slot, 8)
    for copy in zf + lam_copies:
        copy.wait_recv()
    for slot in (0, 1, 3):
        add_cross(slot, 8)
    proj_g(2, 6)
    add_cross(2, 6)
    for half in range(2):
        arrived(half, 2, (6, 7))
    last_g = project(
        jnp.concatenate([rows[pl.ds((half * 4 + 2) * 8 + 6, 2)].reshape(128, BLK) for half in range(2)], axis=0)
    )
    last_a = jnp.concatenate([proj[pl.ds((half * 4 + 2) * 8 + 6, 2)].reshape(128, BLK) for half in range(2)], axis=0)

    total = cnt_ref[0]
    for s in range(1, N_DP):
        total += cnt_ref[s]
    row_total = total.astype(jnp.float32)
    row_a = jnp.sum(lam[0] + lam[1] + lam[2] + lam[3], axis=0, keepdims=True) / row_total
    col_g = jnp.sum(lam_g[...], axis=1, keepdims=True) / row_total
    for part in range(2):
        prows = slice(part * 512, part * 512 + 512)
        value = cross[prows, :] + jnp.dot(last_g[prows], last_a, preferred_element_type=jnp.float32)
        scaled = (value / row_total) / (col_g[prows] * row_a + damping)
        baraw[4 + part * 2 : 6 + part * 2] = scaled.astype(jnp.bfloat16).reshape(2, 256, BLK)

    for copies in (act_copies, p1.values(), p1e.values()):
        for copy in copies:
            copy.wait_send()

    out_copies = []
    for part in range(4):
        prows, cols = pl.ds(part * COLS, COLS), pl.ds(part * COLS, COLS)
        right = jnp.dot(
            bg[prows, :], baraw[pl.ds(4, 4)].reshape(BLK, BLK), preferred_element_type=jnp.float32
        ).astype(jnp.bfloat16)
        sa[:, :, cols] = lax.dot_general(
            basis[...].reshape(BLK, BLK), right, (((1,), (1,)), ((), ())), preferred_element_type=jnp.float32
        ).astype(jnp.bfloat16).reshape(N_DP, 32, COLS)
        for disp in SPREAD:
            i, target = index_of(*disp), at(*disp)
            out_copies.append(
                send(
                    sa.at[target, :, cols], out_hbm.at[me, :, cols],
                    out_send.at[part, i], out_recv.at[part, i], (target, mz),
                )
            )
    own = pltpu.make_async_copy(sa.at[me], out_hbm.at[me], store_sem)
    own.start()
    for copy in out_copies:
        copy.wait_recv()
    own.wait()
    for copy in out_copies + ba_copies + lam_copies + zf + list(z_copies.values()) + list(p2.values()):
        copy.wait_send()


def order_kernel(own_ref, pieces_hbm, out_hbm, sem):
    copies = [
        pltpu.make_async_copy(pieces_hbm.at[own_ref[u]], out_hbm.at[u // 4, u % 4], sem.at[u]) for u in range(N_DP)
    ]
    for copy in copies:
        copy.start()
    for copy in copies:
        copy.wait()


def local(acts, grads_out, counts, owners, bases_a, bases_g):
    smem = pl.BlockSpec(memory_space=pltpu.SMEM)
    hbm = pl.BlockSpec(memory_space=pl.ANY)
    bf16, f32 = jnp.bfloat16, jnp.float32
    dma = pltpu.SemaphoreType.DMA
    pieces = pl.pallas_call(
        kernel,
        out_shape=jax.ShapeDtypeStruct((N_DP, 32, BLK), bf16),
        in_specs=[smem, smem, hbm, hbm, hbm, hbm],
        out_specs=hbm,
        scratch_shapes=[
            pltpu.VMEM((8, 8, 128, HCOL), bf16),
            pltpu.VMEM((8, 2, SUB, BLK), bf16),
            pltpu.VMEM((8, 256, BLK), bf16),
            pltpu.VMEM((BLK, BLK), bf16),
            pltpu.VMEM((2, 3, 8, HALF, BLK), bf16),
            pltpu.VMEM((2, 4, 7, HALF, BLK), bf16),
            pltpu.VMEM((64, HALF, BLK), bf16),
            pltpu.VMEM((N_DP, 32, BLK), bf16),
            pltpu.VMEM((N_DP, 32, BLK), bf16),
            pltpu.VMEM((64, NZ, SUB, BLK), bf16),
            pltpu.VMEM((NZ, 256, BLK), bf16),
            pltpu.VMEM((NZ, 8, BLK), f32),
            pltpu.VMEM((BLK, 128), f32),
            pltpu.VMEM((BLK, BLK), f32),
            pltpu.VMEM((HALF, BLK), bf16),
            pltpu.SMEM((N_DP,), jnp.int32),
            dma((12,)),
            dma((N_DP,)), dma((N_DP,)),
            dma((3,)), dma((3,)),
            dma((3,)), dma((3,)),
            dma((2, 4)), dma((2, 4)),
            dma((2, 4)), dma((2, 4)),
            dma((2, 4, 8)), dma((2, 4, 8)),
            dma((2,)), dma((2,)),
            dma((2,)), dma((2,)),
            dma((4, N_DP)), dma((4, N_DP)),
            dma,
        ],
        compiler_params=pltpu.CompilerParams(
            collective_id=0, has_side_effects=True, vmem_limit_bytes=63 * 1024 * 1024
        ),
        name="kfac",
    )(owners, counts, acts, grads_out, bases_a, bases_g.reshape(BLK, BLK))
    return pl.pallas_call(
        order_kernel,
        out_shape=jax.ShapeDtypeStruct((8, 4, 32, BLK), bf16),
        in_specs=[smem, hbm],
        out_specs=hbm,
        scratch_shapes=[dma((N_DP,))],
        name="order",
    )(owners, pieces)


def solution(mesh):
    placed = (
        P(None, "dp", None),
        P(None, "dp", "mp"),
        P(),
        P(),
        P(None, "mp", None),
        P("mp", "dp", None, None),
    )
    return jax.shard_map(
        local, mesh=mesh, in_specs=placed, out_specs=P(None, "mp", "dp", None), check_vma=False
    )
```

time: 165 us -> 230 us (1.39)
  Pallas kernels: 160 us -> 229 us
  local copies, waits for them, and re-layouts: 3.19 us -> 0 us
    pallas_call x0 -> x1, Pallas kernels: none -> 65.6 us  [local(): pl.pallas_call(order_kernel, out_shape=jax.ShapeDtypeStruct((8, 4, 32, BL...]
    pallas_call x1, Pallas kernels: 160 us -> 163 us  [local(): pl.pallas_call(kernel, out_shape=jax.ShapeDtypeStruct((N_DP, 32, BLK), bf...]
    unnamed x1 -> x0, local copies, waits for them, and re-layouts: 3.19 us -> none
where the time goes in v3:
time: 230 us; the launch traced here: 229 us
  Pallas kernels  229 us (100%)
    pallas_call x1, Pallas kernels, local(): pl.pallas_call(kernel, out_shape=jax.ShapeDtypeStruct((N_DP, 32, BLK), bf...  163 us
    pallas_call x1, Pallas kernels, local(): pl.pallas_call(order_kernel, out_shape=jax.ShapeDtypeStruct((8, 4, 32, BL...  65.6 us

profile of v3, /device:TPU:0, one launch (start us, length us, event | category | flops | bytes accessed | tf_op | source)
XLA Modules:
  0.0 229.0 jit_solution(7747315388137643873)
XLA Ops:
  0.0 163.2 %kfac.1.pieces_hbm = bf16[32,32,1024]{2,1,0:T(8,128)(2,1)} custom-call(s32[32]{0:T(128)} %own_ref.3, s32[32]{0:T(128)} %cnt_ref.1, bf16[8,128,1024]{2,1,0:T(8,128)(2,1)} %acts_hbm.1, bf16[8,128,4096]{2,1,0:T(8,128)(2,1)} %grads_hbm.1, bf16[8,256,1024]{2,1,0:T(8,128)(2,1)} %ba_hbm.1, bf16[1024,1024]{1,0:T(8,128)(2,1)} %bitcast.1), custom_call_target="tpu_custom_call" | custom-call | tf_op jit(solution)/shard_map/kfac/pallas_call | solution.py:323
  163.2 65.6 %order.1 = bf16[8,4,32,1024]{3,2,1,0:T(8,128)(2,1)} custom-call(s32[32]{0:T(128)} %own_ref.3, bf16[32,32,1024]{2,1,0:T(8,128)(2,1)} %kfac.1.pieces_hbm), custom_call_target="tpu_custom_call" | custom-call | tf_op jit(solution)/shard_map/order/pallas_call | solution.py:362

commit v4 on v3

--- a/solution.py
+++ b/solution.py
@@ -28,7 +28,7 @@
     own_ref, cnt_ref, acts_hbm, grads_hbm, ba_hbm, bg_hbm, out_hbm,
     graw, araw, baraw, bg, first, mid, rows, sa, ra, proj, basis, lam, lam_g, cross, mask, inv_ref,
     load_sem, act_send, act_recv, ba_send, ba_recv, lam_send, lam_recv,
-    p1_send, p1_recv, p1e_send, p1e_recv, p2_send, p2_recv, z_send, z_recv, zf_send, zf_recv, out_send, out_recv, store_sem,
+    p1_send, p1_recv, p1e_send, p1e_recv, p2_send, p2_recv, z_send, z_recv, out_send, out_recv, store_sem,
 ):
     me, mz = lax.axis_index("dp"), lax.axis_index("mp")
     my, mx, mc = me // 8, (me // 2) % 4, me % 2
@@ -108,17 +108,31 @@
             block = graw[column * 2 + c, layer, pl.ds(half * HALF, HALF), :]
             dst[:, cols] = block if half == 0 else block * mask[:, cols]
 
-    p1, p1e, p2 = {}, {}, {}
-
-    def forward(half, slot):
-        for e in range(2, 9):
-            e = 1 if e == 8 else e
-            other, dc = SECOND[e]
-            p2[half, slot, e] = send(
-                mid.at[half, slot, e - 1], rows.at[(half * 4 + slot) * 8 + e],
-                p2_send.at[half, slot, e], p2_recv.at[half, slot, e],
-                (at(other, 0, dc) if half == 0 else at(0, other, dc), mz),
-            )
+    p1, p1e = {}, {}
+
+    p2 = []
+
+    def hop_two(half, slot, e, other, dc):
+        return pltpu.make_async_remote_copy(
+            src_ref=mid.at[half, slot, e - 1],
+            dst_ref=rows.at[(half * 4 + slot) * 8 + e],
+            send_sem=p2_send.at[half, slot, e],
+            recv_sem=p2_recv.at[half, slot, e],
+            device_id=(at(other, 0, dc) if half == 0 else at(0, other, dc), mz),
+            device_id_type=MESH,
+        )
+
+    def forward(slot, core):
+        dc = (core + mc) % 2
+        for other in (2, 1, 3):
+            e = jnp.where(dc == 0, SECOND.index((other, 0)), SECOND.index((other, 1)))
+            for half in range(2):
+                p2.append(hop_two(half, slot, e, other, dc))
+                p2[-1].start()
+        if core == 0:
+            for half in range(2):
+                p2.append(hop_two(half, slot, 1, 0, 1))
+                p2[-1].start()
 
     def pack_slot(slot):
         for half in range(2):
@@ -154,7 +168,7 @@
         send(basis.at[mz], basis.at[mz], ba_send.at[k], ba_recv.at[k], zat(dz)) for k, dz in enumerate(SLOTS)
     ]
     forward(0, 0)
-    forward(1, 0)
+    forward(0, 1)
     for slot in SLOTS:
         pack_slot(slot)
         start_slot(slot)
@@ -189,30 +203,51 @@
     lax.fori_loop(0, 2, proj_a_step, 0)
 
     z_copies = {}
-    for k, dz in enumerate((1, 3)):
-        z_copies[dz] = send(proj.at[:, mz], proj.at[:, mz], z_send.at[k], z_recv.at[k], zat(dz))
+
+    def z_send_half(slot, half, owner, k, target):
+        piece = proj.at[pl.ds((half * 4 + slot) * 8, 8), owner]
+        z_copies[slot, k] = send(piece, piece, z_send.at[slot, k], z_recv.at[slot, k], target)
+
+    def z_start(slot):
+        z_send_half(slot, 0, mz, 0, zat(1))
+        z_send_half(slot, 1, mz, 1, zat(3))
+        z_send_half(slot, 1, mz, 2, zat(1))
+        z_send_half(slot, 0, mz, 3, zat(3))
+
+    def z_forward(slot):
+        z_copies[slot, 0].wait_recv()
+        z_send_half(slot, 0, (mz + 3) % NZ, 4, zat(1))
+        z_copies[slot, 1].wait_recv()
+        z_send_half(slot, 1, (mz + 1) % NZ, 5, zat(3))
+
+    z_start(0)
     lam_copies = [send(lam.at[mz], lam.at[mz], lam_send.at[k], lam_recv.at[k], zat(dz)) for k, dz in enumerate(SLOTS)]
-
-    for slot in (1, 3):
+    z_start(1)
+    z_forward(0)
+    z_start(3)
+    z_forward(1)
+    z_start(2)
+
+    def take_slot(slot):
         for half in range(2):
             p1[half, slot].wait_recv()
-            forward(half, slot)
-    for half in range(2):
-        p1[half, 2].wait_recv()
-        forward(half, 2)
-
-    z_copies[1].wait_recv()
-    below = (mz + 3) % NZ
-    zf = [send(proj.at[pl.ds(0, 32), below], proj.at[pl.ds(0, 32), below], zf_send.at[0], zf_recv.at[0], zat(1))]
-    z_copies[3].wait_recv()
-    above = (mz + 1) % NZ
-    zf.append(send(proj.at[pl.ds(32, 32), above], proj.at[pl.ds(32, 32), above], zf_send.at[1], zf_recv.at[1], zat(3)))
+        forward(slot, 0)
+        if slot == 1:
+            forward(slot, 1)
+
+    take_slot(1)
+    z_forward(3)
+    take_slot(3)
+    take_slot(2)
+    forward(3, 1)
+    forward(2, 1)
+    z_forward(2)
 
     def arrived(half, slot, blocks):
         for e in blocks:
             if slot == 0 and e == 0:
                 continue
-            (p1e[half, slot] if e == 0 else p2[half, slot, e]).wait_recv()
+            (p1e[half, slot] if e == 0 else hop_two(half, slot, e, *SECOND[e])).wait_recv()
 
     def project(block):
         value = lax.dot_general(
@@ -248,21 +283,34 @@
 
         lax.fori_loop(0, 4, step, 0)
 
+    def z_arrived(slot):
+        for k in range(2, 6):
+            z_copies[slot, k].wait_recv()
+
     for slot in (0, 1, 3):
         proj_g(slot, 8)
-    for copy in zf + lam_copies:
+        z_arrived(slot)
+        add_cross(slot, 8)
+    proj_g(2, 4)
+    z_arrived(2)
+    add_cross(2, 4)
+
+    def pair(e):
+        for half in range(2):
+            arrived(half, 2, (e, e + 1))
+        starts = [(half * 4 + 2) * 8 + e for half in range(2)]
+        block = jnp.concatenate([rows[b : b + 2].reshape(128, BLK) for b in starts], axis=0)
+        right = jnp.concatenate([proj[b : b + 2].reshape(128, BLK) for b in starts], axis=0)
+        return project(block), right
+
+    pair_g, pair_a = pair(4)
+    for part in range(2):
+        prows = slice(part * 512, part * 512 + 512)
+        cross[prows, :] += jnp.dot(pair_g[prows], pair_a, preferred_element_type=jnp.float32)
+    last_g, last_a = pair(6)
+
+    for copy in lam_copies:
         copy.wait_recv()
-    for slot in (0, 1, 3):
-        add_cross(slot, 8)
-    proj_g(2, 6)
-    add_cross(2, 6)
-    for half in range(2):
-        arrived(half, 2, (6, 7))
-    last_g = project(
-        jnp.concatenate([rows[pl.ds((half * 4 + 2) * 8 + 6, 2)].reshape(128, BLK) for half in range(2)], axis=0)
-    )
-    last_a = jnp.concatenate([proj[pl.ds((half * 4 + 2) * 8 + 6, 2)].reshape(128, BLK) for half in range(2)], axis=0)
-
     total = cnt_ref[0]
     for s in range(1, N_DP):
         total += cnt_ref[s]
@@ -301,17 +349,21 @@
     for copy in out_copies:
         copy.wait_recv()
     own.wait()
-    for copy in out_copies + ba_copies + lam_copies + zf + list(z_copies.values()) + list(p2.values()):
+    for copy in out_copies + ba_copies + lam_copies + list(z_copies.values()) + p2:
         copy.wait_send()
 
 
-def order_kernel(own_ref, pieces_hbm, out_hbm, sem):
-    copies = [
-        pltpu.make_async_copy(pieces_hbm.at[own_ref[u]], out_hbm.at[u // 4, u % 4], sem.at[u]) for u in range(N_DP)
-    ]
-    for copy in copies:
+def order_kernel(own_ref, pieces_hbm, out_hbm, held, load_sem, store_sem):
+    loads = [pltpu.make_async_copy(pieces_hbm.at[own_ref[u]], held.at[u], load_sem.at[u]) for u in range(N_DP)]
+    for copy in loads:
         copy.start()
-    for copy in copies:
+    stores = []
+    for layer in range(8):
+        for copy in loads[layer * 4 : layer * 4 + 4]:
+            copy.wait()
+        stores.append(pltpu.make_async_copy(held.at[pl.ds(layer * 4, 4)], out_hbm.at[layer], store_sem.at[layer]))
+        stores[-1].start()
+    for copy in stores:
         copy.wait()
 
 
@@ -349,8 +401,7 @@
             dma((2, 4)), dma((2, 4)),
             dma((2, 4)), dma((2, 4)),
             dma((2, 4, 8)), dma((2, 4, 8)),
-            dma((2,)), dma((2,)),
-            dma((2,)), dma((2,)),
+            dma((4, 6)), dma((4, 6)),
             dma((4, N_DP)), dma((4, N_DP)),
             dma,
         ],
@@ -364,7 +415,7 @@
         out_shape=jax.ShapeDtypeStruct((8, 4, 32, BLK), bf16),
         in_specs=[smem, hbm],
         out_specs=hbm,
-        scratch_shapes=[dma((N_DP,))],
+        scratch_shapes=[pltpu.VMEM((N_DP, 32, BLK), bf16), dma((N_DP,)), dma((8,))],
         name="order",
     )(owners, pieces)
 

time: 230 us -> 158 us (0.69)
  Pallas kernels: 229 us -> 158 us
    pallas_call x1, Pallas kernels: 65.6 us -> 3.31 us  [local(): pl.pallas_call(order_kernel, out_shape=jax.ShapeDtypeStruct((8, 4, 32, BL...]
    pallas_call x1, Pallas kernels: 163 us -> 154 us  [local(): pl.pallas_call(kernel, out_shape=jax.ShapeDtypeStruct((N_DP, 32, BLK), bf...]
where the time goes in v4:
time: 158 us
  Pallas kernels  158 us (100%)
    pallas_call x1, Pallas kernels, local(): pl.pallas_call(kernel, out_shape=jax.ShapeDtypeStruct((N_DP, 32, BLK), bf...  154 us
    pallas_call x1, Pallas kernels, local(): pl.pallas_call(order_kernel, out_shape=jax.ShapeDtypeStruct((8, 4, 32, BL...  3.31 us

profile of v4, /device:TPU:0, one launch (start us, length us, event | category | flops | bytes accessed | tf_op | source)
XLA Modules:
  0.0 157.9 jit_solution(6984642335241525954)
XLA Ops:
  0.0 154.4 %kfac.1.pieces_hbm = bf16[32,32,1024]{2,1,0:T(8,128)(2,1)} custom-call(s32[32]{0:T(128)} %own_ref.3, s32[32]{0:T(128)} %cnt_ref.1, bf16[8,128,1024]{2,1,0:T(8,128)(2,1)} %acts_hbm.1, bf16[8,128,4096]{2,1,0:T(8,128)(2,1)} %grads_hbm.1, bf16[8,256,1024]{2,1,0:T(8,128)(2,1)} %ba_hbm.1, bf16[1024,1024]{1,0:T(8,128)(2,1)} %bitcast.1), custom_call_target="tpu_custom_call" | custom-call | tf_op jit(solution)/shard_map/kfac/pallas_call | solution.py:375
  154.5 3.3 %order.1 = bf16[8,4,32,1024]{3,2,1,0:T(8,128)(2,1)} custom-call(s32[32]{0:T(128)} %own_ref.3, bf16[32,32,1024]{2,1,0:T(8,128)(2,1)} %kfac.1.pieces_hbm), custom_call_target="tpu_custom_call" | custom-call | tf_op jit(solution)/shard_map/order/pallas_call | solution.py:413

commit v5 on v4

--- a/solution.py
+++ b/solution.py
@@ -46,23 +46,23 @@
         copy.start()
         return copy
 
+    barrier = pltpu.get_barrier_semaphore()
+    peers = [(at(*d), mz) for d in SPREAD] + [zat(dz) for dz in (1, 2, 3)]
+    for peer in peers:
+        pl.semaphore_signal(barrier, inc=1, device_id=peer, device_id_type=MESH)
+
     loads = [
         pltpu.make_async_copy(acts_hbm.at[:, pl.ds(mz * SUB, SUB)], araw.at[:, 0], load_sem.at[0]),
         pltpu.make_async_copy(acts_hbm.at[:, pl.ds(HALF + mz * SUB, SUB)], araw.at[:, 1], load_sem.at[1]),
     ]
+    loads.append(pltpu.make_async_copy(ba_hbm, baraw, load_sem.at[10]))
     for j in range(8):
         loads.append(
             pltpu.make_async_copy(grads_hbm.at[:, :, pl.ds(j * HCOL, HCOL)], graw.at[j], load_sem.at[2 + j])
         )
-    loads.append(pltpu.make_async_copy(ba_hbm, baraw, load_sem.at[10]))
     loads.append(pltpu.make_async_copy(bg_hbm, bg, load_sem.at[11]))
     for copy in loads:
         copy.start()
-
-    barrier = pltpu.get_barrier_semaphore()
-    peers = [(at(*d), mz) for d in SPREAD] + [zat(dz) for dz in (1, 2, 3)]
-    for peer in peers:
-        pl.semaphore_signal(barrier, inc=1, device_id=peer, device_id_type=MESH)
 
     def invert(d, carry):
         unit = jnp.int32(0)
@@ -92,6 +92,18 @@
     for disp in SPREAD:
         pack_acts(sa, index_of(*disp), disp)
     pack_acts(ra, 0, (0, 0, 0))
+
+    pl.semaphore_wait(barrier, len(peers))
+    act_copies = []
+    for disp in SPREAD:
+        i = index_of(*disp)
+        act_copies.append(send(sa.at[i], ra.at[i], act_send.at[i], act_recv.at[i], (at(*disp), mz)))
+
+    loads[2].wait()
+    basis[mz] = baraw[inv_ref[me] // 4]
+    ba_copies = [
+        send(basis.at[mz], basis.at[mz], ba_send.at[k], ba_recv.at[k], zat(dz)) for k, dz in enumerate(SLOTS)
+    ]
 
     def disp_of(half, slot, e):
         other, dc = SECOND[e]
@@ -151,22 +163,11 @@
             )
 
     for j in range(8):
-        loads[2 + j].wait()
+        loads[3 + j].wait()
     for half in range(2):
         for e in range(1, 8):
             pack(mid.at[half, 0, e - 1], half, disp_of(half, 0, e))
         pack(rows.at[half * 32], half, disp_of(half, 0, 0))
-    loads[10].wait()
-    basis[mz] = baraw[inv_ref[me] // 4]
-
-    pl.semaphore_wait(barrier, len(peers))
-    act_copies = []
-    for disp in SPREAD:
-        i = index_of(*disp)
-        act_copies.append(send(sa.at[i], ra.at[i], act_send.at[i], act_recv.at[i], (at(*disp), mz)))
-    ba_copies = [
-        send(basis.at[mz], basis.at[mz], ba_send.at[k], ba_recv.at[k], zat(dz)) for k, dz in enumerate(SLOTS)
-    ]
     forward(0, 0)
     forward(0, 1)
     for slot in SLOTS:
@@ -232,13 +233,13 @@
         for half in range(2):
             p1[half, slot].wait_recv()
         forward(slot, 0)
-        if slot == 1:
-            forward(slot, 1)
+
 
     take_slot(1)
     z_forward(3)
     take_slot(3)
     take_slot(2)
+    forward(1, 1)
     forward(3, 1)
     forward(2, 1)
     z_forward(2)

time: 158 us -> 157 us (level)
  Pallas kernels: 158 us -> 156 us
where the time goes in v5:
time: 157 us
  Pallas kernels  156 us (99%)
    pallas_call x1, Pallas kernels, local(): pl.pallas_call(kernel, out_shape=jax.ShapeDtypeStruct((N_DP, 32, BLK), bf...  153 us
    pallas_call x1, Pallas kernels, local(): pl.pallas_call(order_kernel, out_shape=jax.ShapeDtypeStruct((8, 4, 32, BL...  3.31 us

profile of v5, /device:TPU:0, one launch (start us, length us, event | category | flops | bytes accessed | tf_op | source)
XLA Modules:
  0.0 156.5 jit_solution(10018772451269689646)
XLA Ops:
  0.0 153.1 %kfac.1.pieces_hbm = bf16[32,32,1024]{2,1,0:T(8,128)(2,1)} custom-call(s32[32]{0:T(128)} %own_ref.3, s32[32]{0:T(128)} %cnt_ref.1, bf16[8,128,1024]{2,1,0:T(8,128)(2,1)} %acts_hbm.1, bf16[8,128,4096]{2,1,0:T(8,128)(2,1)} %grads_hbm.1, bf16[8,256,1024]{2,1,0:T(8,128)(2,1)} %ba_hbm.1, bf16[1024,1024]{1,0:T(8,128)(2,1)} %bitcast.1), custom_call_target="tpu_custom_call" | custom-call | tf_op jit(solution)/shard_map/kfac/pallas_call | solution.py:376
  153.1 3.3 %order.1 = bf16[8,4,32,1024]{3,2,1,0:T(8,128)(2,1)} custom-call(s32[32]{0:T(128)} %own_ref.3, bf16[32,32,1024]{2,1,0:T(8,128)(2,1)} %kfac.1.pieces_hbm), custom_call_target="tpu_custom_call" | custom-call | tf_op jit(solution)/shard_map/order/pallas_call | solution.py:414

commit v6 on v5

--- a/solution.py
+++ b/solution.py
@@ -243,6 +243,9 @@
     forward(3, 1)
     forward(2, 1)
     z_forward(2)
+    for copies in (act_copies, ba_copies, lam_copies):
+        for copy in copies:
+            copy.wait_send()
 
     def arrived(half, slot, blocks):
         for e in blocks:
@@ -296,19 +299,11 @@
     z_arrived(2)
     add_cross(2, 4)
 
-    def pair(e):
-        for half in range(2):
-            arrived(half, 2, (e, e + 1))
-        starts = [(half * 4 + 2) * 8 + e for half in range(2)]
-        block = jnp.concatenate([rows[b : b + 2].reshape(128, BLK) for b in starts], axis=0)
-        right = jnp.concatenate([proj[b : b + 2].reshape(128, BLK) for b in starts], axis=0)
-        return project(block), right
-
-    pair_g, pair_a = pair(4)
-    for part in range(2):
-        prows = slice(part * 512, part * 512 + 512)
-        cross[prows, :] += jnp.dot(pair_g[prows], pair_a, preferred_element_type=jnp.float32)
-    last_g, last_a = pair(6)
+    for half in range(2):
+        arrived(half, 2, range(4, 8))
+    starts = [(half * 4 + 2) * 8 + 4 for half in range(2)]
+    last_a = jnp.concatenate([proj[b : b + 4].reshape(256, BLK) for b in starts], axis=0)
+    last_g = project(jnp.concatenate([rows[b : b + 4].reshape(256, BLK) for b in starts], axis=0))
 
     for copy in lam_copies:
         copy.wait_recv()
@@ -323,10 +318,6 @@
         value = cross[prows, :] + jnp.dot(last_g[prows], last_a, preferred_element_type=jnp.float32)
         scaled = (value / row_total) / (col_g[prows] * row_a + damping)
         baraw[4 + part * 2 : 6 + part * 2] = scaled.astype(jnp.bfloat16).reshape(2, 256, BLK)
-
-    for copies in (act_copies, p1.values(), p1e.values()):
-        for copy in copies:
-            copy.wait_send()
 
     out_copies = []
     for part in range(4):
@@ -347,11 +338,12 @@
             )
     own = pltpu.make_async_copy(sa.at[me], out_hbm.at[me], store_sem)
     own.start()
+    for copies in (p1.values(), p1e.values(), z_copies.values(), p2):
+        for copy in copies:
+            copy.wait_send()
+    own.wait()
     for copy in out_copies:
-        copy.wait_recv()
-    own.wait()
-    for copy in out_copies + ba_copies + lam_copies + list(z_copies.values()) + p2:
-        copy.wait_send()
+        copy.wait()
 
 
 def order_kernel(own_ref, pieces_hbm, out_hbm, held, load_sem, store_sem):

time: 157 us -> 155 us (0.987)
    pallas_call x1, Pallas kernels: 153 us -> 151 us  [local(): pl.pallas_call(kernel, out_shape=jax.ShapeDtypeStruct((N_DP, 32, BLK), bf...]
where the time goes in v6:
time: 155 us
  Pallas kernels  155 us (100%)
    pallas_call x1, Pallas kernels, local(): pl.pallas_call(kernel, out_shape=jax.ShapeDtypeStruct((N_DP, 32, BLK), bf...  151 us
    pallas_call x1, Pallas kernels, local(): pl.pallas_call(order_kernel, out_shape=jax.ShapeDtypeStruct((8, 4, 32, BL...  3.31 us

profile of v6, /device:TPU:0, one launch (start us, length us, event | category | flops | bytes accessed | tf_op | source)
XLA Modules:
  0.0 154.8 jit_solution(3443103899956633698)
XLA Ops:
  0.0 151.3 %kfac.1.pieces_hbm = bf16[32,32,1024]{2,1,0:T(8,128)(2,1)} custom-call(s32[32]{0:T(128)} %own_ref.3, s32[32]{0:T(128)} %cnt_ref.1, bf16[8,128,1024]{2,1,0:T(8,128)(2,1)} %acts_hbm.1, bf16[8,128,4096]{2,1,0:T(8,128)(2,1)} %grads_hbm.1, bf16[8,256,1024]{2,1,0:T(8,128)(2,1)} %ba_hbm.1, bf16[1024,1024]{1,0:T(8,128)(2,1)} %bitcast.1), custom_call_target="tpu_custom_call" | custom-call | tf_op jit(solution)/shard_map/kfac/pallas_call | solution.py:368
  151.3 3.3 %order.1 = bf16[8,4,32,1024]{3,2,1,0:T(8,128)(2,1)} custom-call(s32[32]{0:T(128)} %own_ref.3, bf16[32,32,1024]{2,1,0:T(8,128)(2,1)} %kfac.1.pieces_hbm), custom_call_target="tpu_custom_call" | custom-call | tf_op jit(solution)/shard_map/order/pallas_call | solution.py:406

commit v7 on v6

--- a/solution.py
+++ b/solution.py
@@ -169,10 +169,10 @@
             pack(mid.at[half, 0, e - 1], half, disp_of(half, 0, e))
         pack(rows.at[half * 32], half, disp_of(half, 0, 0))
     forward(0, 0)
-    forward(0, 1)
     for slot in SLOTS:
         pack_slot(slot)
         start_slot(slot)
+    forward(0, 1)
 
     loads[11].wait()
     for k in range(4):
@@ -295,16 +295,6 @@
         proj_g(slot, 8)
         z_arrived(slot)
         add_cross(slot, 8)
-    proj_g(2, 4)
-    z_arrived(2)
-    add_cross(2, 4)
-
-    for half in range(2):
-        arrived(half, 2, range(4, 8))
-    starts = [(half * 4 + 2) * 8 + 4 for half in range(2)]
-    last_a = jnp.concatenate([proj[b : b + 4].reshape(256, BLK) for b in starts], axis=0)
-    last_g = project(jnp.concatenate([rows[b : b + 4].reshape(256, BLK) for b in starts], axis=0))
-
     for copy in lam_copies:
         copy.wait_recv()
     total = cnt_ref[0]
@@ -312,6 +302,16 @@
         total += cnt_ref[s]
     row_total = total.astype(jnp.float32)
     row_a = jnp.sum(lam[0] + lam[1] + lam[2] + lam[3], axis=0, keepdims=True) / row_total
+    proj_g(2, 4)
+    z_arrived(2)
+    add_cross(2, 4)
+
+    for half in range(2):
+        arrived(half, 2, range(4, 8))
+    starts = [(half * 4 + 2) * 8 + 4 for half in range(2)]
+    last_a = jnp.concatenate([proj[b : b + 4].reshape(256, BLK) for b in starts], axis=0)
+    last_g = project(jnp.concatenate([rows[b : b + 4].reshape(256, BLK) for b in starts], axis=0))
+
     col_g = jnp.sum(lam_g[...], axis=1, keepdims=True) / row_total
     for part in range(2):
         prows = slice(part * 512, part * 512 + 512)

time: 155 us -> 155 us (level)
  no operation moved by 1% of the time
where the time goes in v7:
time: 155 us; the launch traced here: 154 us
  Pallas kernels  154 us (99%)
    pallas_call x1, Pallas kernels, local(): pl.pallas_call(kernel, out_shape=jax.ShapeDtypeStruct((N_DP, 32, BLK), bf...  151 us
    pallas_call x1, Pallas kernels, local(): pl.pallas_call(order_kernel, out_shape=jax.ShapeDtypeStruct((8, 4, 32, BL...  3.31 us

profile of v7, /device:TPU:0, one launch (start us, length us, event | category | flops | bytes accessed | tf_op | source)
XLA Modules:
  0.0 154.3 jit_solution(1151501593001842722)
XLA Ops:
  0.0 150.8 %kfac.1.pieces_hbm = bf16[32,32,1024]{2,1,0:T(8,128)(2,1)} custom-call(s32[32]{0:T(128)} %own_ref.3, s32[32]{0:T(128)} %cnt_ref.1, bf16[8,128,1024]{2,1,0:T(8,128)(2,1)} %acts_hbm.1, bf16[8,128,4096]{2,1,0:T(8,128)(2,1)} %grads_hbm.1, bf16[8,256,1024]{2,1,0:T(8,128)(2,1)} %ba_hbm.1, bf16[1024,1024]{1,0:T(8,128)(2,1)} %bitcast.1), custom_call_target="tpu_custom_call" | custom-call | tf_op jit(solution)/shard_map/kfac/pallas_call | solution.py:368
  150.8 3.3 %order.1 = bf16[8,4,32,1024]{3,2,1,0:T(8,128)(2,1)} custom-call(s32[32]{0:T(128)} %own_ref.3, bf16[32,32,1024]{2,1,0:T(8,128)(2,1)} %kfac.1.pieces_hbm), custom_call_target="tpu_custom_call" | custom-call | tf_op jit(solution)/shard_map/order/pallas_call | solution.py:406
